TPU v7x, 128 devices: a whole 4x4x4 slice. The times are simulated.
128 devices in a mesh: dp: 64 (over x_hi, y, z, core), sub: 2 (over x_lo).
Axes of the slice: x: 4 (x_hi: 2, x_lo: 2; x = x_hi * 2 + x_lo), y: 4, z: 4, core: 2. Of those that a mesh axis runs over, the one named last changes fastest.
Arguments:
- images: bfloat16 [65536, 1152], P(('dp', 'sub')), may hold values from -1 to 1
- text_embeds: bfloat16 [65536, 1152], P('dp'), may hold values from -3 to 3
- dest_slot: int32 [65536], P(('dp', 'sub')), may hold values from -1 to 32767, as said below
- labels: int32 [32768], P(('dp', 'sub')), may hold values from 0 to 65535, as said below
- logit_scale: float32 [1], replicated, may hold values from 2 to 6
- logit_bias: float32 [1], replicated, may hold values from -3 to -1
Outputs:
- grad_images: bfloat16 [65536, 1152], P(('dp', 'sub'))
- grad_text: float32 [65536, 1152], P(('dp', 'sub'))
- loss: float32 [1], replicated
- grad_scale: float32 [1], replicated
- grad_bias: float32 [1], replicated
Inputs may be any that keep to these rules, and one draw needn't show every extreme that they name: `dest_slot`: every slot is named by exactly one packed row. At most 4 packed rows of one device name slots of one device, and every device receives exactly 4 rows from half of the devices; one device has no padding rows. labels[i] names a text whose block is (i // 512 - s) mod 64 for some s in 0 .. 3.
All inputs are finite; a program needn't handle non-finite values.
Results may differ from a plain program's by a relative error of at most 0.0034.
Values may be sent and summed in bfloat16 or wider, within the bound.
A program may use at most 128 MiB of HBM per device.

v0:
```python
import jax
import jax.numpy as jnp
from jax import lax
from jax.sharding import PartitionSpec as P

STOPS = 4


def from_behind(block, axis, distance):
    devices = range(lax.axis_size(axis))
    route = [((i - distance) % len(devices), i) for i in devices]
    return lax.ppermute(block, axis, route)


def pair_terms(slot_rows, slot_labels, block_rows, owner_block, factor, offset):
    txt_rows = block_rows.shape[0]
    text_ids_local = jnp.arange(txt_rows)
    inner = jnp.dot(slot_rows, block_rows.T, preferred_element_type=jnp.float32)
    logits = factor * inner + offset
    positive = slot_labels[:, None] == (owner_block * txt_rows + text_ids_local)[None, :]
    label_sign = jnp.where(positive, 1.0, -1.0).astype(jnp.float32)
    loss_sum = -jnp.sum(jax.nn.log_sigmoid(label_sign * logits))
    logit_grad = jax.nn.sigmoid(logits) - positive.astype(jnp.float32)
    scale_sum = jnp.sum(logit_grad * inner)
    bias_sum = jnp.sum(logit_grad)
    weights = logit_grad.astype(jnp.bfloat16)
    image_term = jnp.dot(weights, block_rows, preferred_element_type=jnp.float32)
    text_term = jnp.dot(weights.T, slot_rows, preferred_element_type=jnp.float32)
    return (image_term, text_term, loss_sum, scale_sum, bias_sum)


def local(images, text_embeds, dest_slot, labels, logit_scale, logit_bias):
    dp_count = lax.axis_size("dp")
    sub_count = lax.axis_size("sub")
    devices = dp_count * sub_count
    capacity = images.shape[0]
    pair_cap = capacity // devices
    slots_here = labels.shape[0]
    columns = images.shape[1]
    txt_rows = text_embeds.shape[0]
    occupied = dest_slot >= 0
    target = jnp.where(occupied, dest_slot // slots_here, devices)
    local_slot = jnp.where(occupied, dest_slot % slots_here, slots_here)
    onehot = (target[:, None] == jnp.arange(devices)[None, :]).astype(jnp.int32)
    ranking = jnp.cumsum(onehot, axis=0) - 1
    within = jnp.sum(onehot * ranking, axis=1)
    placed = target * pair_cap + within
    outgoing = (
        jnp.zeros((devices * pair_cap, columns), jnp.bfloat16).at[placed].set(images, mode="drop")
    )
    out_ids = (
        jnp.full((devices * pair_cap,), slots_here, jnp.int32)
        .at[placed]
        .set(local_slot, mode="drop")
    )
    arrived, arrived_ids = (
        lax.all_to_all(
            outgoing.reshape(devices, pair_cap, columns),
            ("dp", "sub"),
            split_axis=0,
            concat_axis=0,
            tiled=True,
        ),
        lax.all_to_all(
            out_ids.reshape(devices, pair_cap),
            ("dp", "sub"),
            split_axis=0,
            concat_axis=0,
            tiled=True,
        ),
    )
    arrived_ids = arrived_ids.reshape(-1)
    slotted = (
        jnp.zeros((slots_here, columns), jnp.bfloat16)
        .at[arrived_ids]
        .set(arrived.reshape(-1, columns), mode="drop")
    )
    here_index = lax.axis_index("dp")
    factor = logit_scale[0]
    offset = logit_bias[0]
    current = text_embeds
    for visit in range(STOPS):
        if visit > 0:
            current = from_behind(current, "dp", 1)
            text_sum = from_behind(text_sum, "dp", 1)
        owner_block = (here_index - visit) % dp_count
        image_term, text_term, loss_sum, scale_sum, bias_sum = pair_terms(
            slotted, labels, current, owner_block, factor, offset
        )
        if visit == 0:
            image_sum = image_term
            text_sum = text_term
            loss_total = loss_sum
            scale_total = scale_sum
            bias_total = bias_sum
        else:
            image_sum = image_sum + image_term
            loss_total = loss_total + loss_sum
            scale_total = scale_total + scale_sum
            bias_total = bias_total + bias_sum
            text_sum = text_sum + text_term
    text_sum = from_behind(text_sum, "dp", 1 - STOPS)
    halves = lax.psum_scatter(text_sum, "sub", scatter_dimension=0, tiled=True)
    grad_text = factor * halves
    loss_all, scale_all, bias_all = lax.psum((loss_total, scale_total, bias_total), ("dp", "sub"))
    pair_count = float(slots_here * devices * STOPS * txt_rows)
    slot_grad = (factor * image_sum).astype(jnp.bfloat16)
    usable = arrived_ids < slots_here
    picked = jnp.take(slot_grad, jnp.minimum(arrived_ids, slots_here - 1), axis=0)
    returning = jnp.where(usable[:, None], picked, jnp.zeros_like(picked))
    returned = lax.all_to_all(
        returning.reshape(devices, pair_cap, columns),
        ("dp", "sub"),
        split_axis=0,
        concat_axis=0,
        tiled=True,
    )
    returned = returned.reshape(-1, columns)
    fetched = jnp.take(returned, jnp.minimum(placed, devices * pair_cap - 1), axis=0)
    grad_images = jnp.where(occupied[:, None], fetched, jnp.zeros_like(fetched))
    loss = (loss_all / pair_count).reshape(1)
    grad_scale = (scale_all / pair_count).reshape(1)
    grad_bias = (bias_all / pair_count).reshape(1)
    return (grad_images, grad_text, loss, grad_scale, grad_bias)


def solution(mesh):
    return jax.shard_map(
        local,
        mesh=mesh,
        in_specs=(
            P(("dp", "sub"), None),
            P("dp", None),
            P(("dp", "sub")),
            P(("dp", "sub")),
            P(),
            P(),
        ),
        out_specs=(P(("dp", "sub"), None), P(("dp", "sub"), None), P(), P(), P()),
        check_vma=False,
    )
```

profile of v0, /device:TPU:1, one launch (start us, length us, event | category | flops | bytes accessed | tf_op | source)
XLA Modules:
  0.0 574.6 jit_solution(12443935250602985021)
XLA Ops:
  8.6 2.4 scatter_custom_fusion
  11.8 11.5 %all-to-all-start = ((s32[128,1,4]{2,1,0:T(1,128)}), s32[128,1,4]{2,1,0:T(1,128)S(1)}, u32[]{:S(2)}, u32[]{:S(2)}) async-start(s32[128,1,4]{2,1,0:T(1,128)} %bitcast.4), calls=%async_computation | async-start | bytes 131072 | tf_op jit(solution)/shard_map/all_to_all | solution.py:64
  23.3 3.8 scatter_custom_fusion.1
  28.2 4.6 all-to-all-done
  32.8 5.2 all-to-all-start.1
  40.9 17.6 %all-to-all-done.1 = bf16[128,4,1152]{2,1,0:T(4,128)(2,1)S(1)} async-done(((bf16[128,4,1152]{2,1,0:T(4,128)(2,1)}), bf16[128,4,1152]{2,1,0:T(4,128)(2,1)S(1)}, u32[]{:S(2)}, u32[]{:S(2)}) %all-to-all-start.1) | async-done | bytes 1179680 | tf_op jit(solution)/shard_map/all_to_all | solution.py:57
  58.8 2.8 scatter_custom_fusion.2
  61.6 2.5 fusion.55
  64.2 3.3 fusion.31
  67.9 76.6 %collective-permute-done = bf16[1024,1152]{1,0:T(8,128)(2,1)} collective-permute-done((bf16[1024,1152]{1,0:T(8,128)(2,1)}, bf16[1024,1152]{1,0:T(8,128)(2,1)}, u32[]{:S(2)}, u32[]{:S(2)}) %collective-permute-start) | collective-permute-done | bytes 2359328 | tf_op jit(solution)/shard_map/ppermute | solution.py:12
  144.4 2.5 fusion.56
  147.0 5.7 convolution_add_fusion
  152.6 2.5 collective-permute-start.4
  155.1 76.6 %collective-permute-done.1 = bf16[1024,1152]{1,0:T(8,128)(2,1)} collective-permute-done((bf16[1024,1152]{1,0:T(8,128)(2,1)}, bf16[1024,1152]{1,0:T(8,128)(2,1)}, u32[]{:S(2)}, u32[]{:S(2)}) %collective-permute-start.1) | collective-permute-done | bytes 2359328 | tf_op jit(solution)/shard_map/ppermute | solution.py:12
  231.8 2.5 fusion.57
  235.4 5.2 add.239
  240.6 2.5 collective-permute-start.5
  243.2 76.6 %collective-permute-done.2 = bf16[1024,1152]{1,0:T(8,128)(2,1)} collective-permute-done((bf16[1024,1152]{1,0:T(8,128)(2,1)}, bf16[1024,1152]{1,0:T(8,128)(2,1)}, u32[]{:S(2)}, u32[]{:S(2)}) %collective-permute-start.2) | collective-permute-done | bytes 2359328 | tf_op jit(solution)/shard_map/ppermute | solution.py:12
  319.8 7.7 %fusion.44 = (f32[]{:T(128)}, f32[]{:T(128)}, f32[]{:T(128)}, f32[]{:T(128)}, f32[]{:T(128)}, /*index=5*/f32[]{:T(128)}, f32[]{:T(128)}, f32[]{:T(128)}, f32[]{:...) fusion(s32[1024]{0:T(1024)S(1)} %iota_add_fusion, s32[256]{0:T(256)S(1)} %copy-done.3, ...), kind=kOutput, calls=%fused_computation.104 | convolution fusion | flops 625999872 | bytes 7160888 | tf_op jit(solution)/shard_map/dot_general | solution.py:18
  328.6 3.0 add.240
  331.6 4.4 collective-permute-start.6
  336.0 87.7 %collective-permute-done.6 = f32[1024,1152]{1,0:T(8,128)} collective-permute-done((f32[1024,1152]{1,0:T(8,128)S(1)}, f32[1024,1152]{1,0:T(8,128)}, u32[]{:S(2)}, u32[]{:S(2)}) %collective-permute-start.6) | collective-permute-done | bytes 4718624 | tf_op jit(solution)/shard_map/ppermute | solution.py:12
  424.0 2.6 fusion.33
  426.7 2.7 convolution_add_fusion.3
  429.4 2.7 convolution_add_fusion.2
  432.2 2.6 fusion.1
  434.8 2.1 gather_fusion
  437.3 1.8 select_select_fusion.1
  439.1 31.4 %all-to-all-start.2 = ((bf16[128,4,1152]{2,1,0:T(4,128)(2,1)}), bf16[128,4,1152]{2,1,0:T(4,128)(2,1)S(1)}, u32[]{:S(2)}, u32[]{:S(2)}) async-start(bf16[128,4,1152]{2,1,0:T(4,128)(2,1)} %select_select_fusion.1), calls=%async_computation.2 | async-start | bytes 2359296 | tf_op jit(solution)/shard_map/all_to_all | solution.py:111
  478.3 77.1 %all-reduce = (f32[]{:T(128)}, f32[]{:T(128)}, f32[]{:T(128)}) all-reduce(f32[]{:T(128)S(6)} %add.247, f32[]{:T(128)S(6)} %add.250, f32[]{:T(128)S(6)} %add.253), channel_id=1, replica_groups=mesh['dp'=64,'sub'=2] {'dp','sub'}, use_global_device_ids=true, to_apply=%region_11.12 | all-reduce | flops 3 | bytes 24 | tf_op jit(solution)/shard_map/psum | solution.py:105
  557.7 2.1 gather_fusion.1
  561.1 3.2 broadcast_multiply_fusion
  (57 shorter events, 9.9 us)
Async XLA Ops:
  11.8 21.1 %all-to-all-start = ((s32[128,1,4]{2,1,0:T(1,128)}), s32[128,1,4]{2,1,0:T(1,128)S(1)}, u32[]{:S(2)}, u32[]{:S(2)}) async-start(s32[128,1,4]{2,1,0:T(1,128)} %bitcast.4), calls=%async_computation | async-start | bytes 131072 | tf_op jit(solution)/shard_map/all_to_all | solution.py:64
  32.8 25.6 %all-to-all-start.1 = ((bf16[128,4,1152]{2,1,0:T(4,128)(2,1)}), bf16[128,4,1152]{2,1,0:T(4,128)(2,1)S(1)}, u32[]{:S(2)}, u32[]{:S(2)}) async-start(bf16[128,4,1152]{2,1,0:T(4,128)(2,1)} %reshape.156), calls=%async_computation.1 | async-start | bytes 2359296 | tf_op jit(solution)/shard_map/all_to_all | solution.py:57
  38.0 523.1 %reduce-scatter.2.cloned.1.call-start = ((), (), s32[]{:S(2)}) async-start(), calls=%async_computation.4 | async-start | bytes 7077888 | tf_op jit(solution)/shard_map/reduce_scatter | solution.py:103
  61.6 2.6 copy-start.3
  67.5 79.5 %collective-permute-start.3 = (f32[1024,1152]{1,0:T(8,128)}, f32[1024,1152]{1,0:T(8,128)}, u32[]{:S(2)}, u32[]{:S(2)}) collective-permute-start(f32[1024,1152]{1,0:T(8,128)} %fusion.31), channel_id=1, source_target_pairs={{126,0},{0,2},{2,4},{4,6},{6,8},{8,10},{10,12},{12,14},{14,16},{16... | collective-permute-start | bytes 14155784 | tf_op jit(solution)/shard_map/ppermute | solution.py:12
  67.7 76.7 %collective-permute-start = (bf16[1024,1152]{1,0:T(8,128)(2,1)}, bf16[1024,1152]{1,0:T(8,128)(2,1)}, u32[]{:S(2)}, u32[]{:S(2)}) collective-permute-start(bf16[1024,1152]{1,0:T(8,128)(2,1)} %param.7), channel_id=1, source_target_pairs={{126,0},{0,2},{2,4},{4,6},{6,8},{8,10},{10,12},{12,14},{14,16},{16... | collective-permute-start | bytes 7077896 | tf_op jit(solution)/shard_map/ppermute | solution.py:12
  152.6 82.8 %collective-permute-start.4 = (f32[1024,1152]{1,0:T(8,128)}, f32[1024,1152]{1,0:T(8,128)}, u32[]{:S(2)}, u32[]{:S(2)}) collective-permute-start(f32[1024,1152]{1,0:T(8,128)} %convolution_add_fusion), channel_id=1, source_target_pairs={{126,0},{0,2},{2,4},{4,6},{6,8},{8,10},{10,12},{12,14},{14,16},{16... | collective-permute-start | bytes 14155784 | tf_op jit(solution)/shard_map/ppermute | solution.py:12
  155.1 76.7 %collective-permute-start.1 = (bf16[1024,1152]{1,0:T(8,128)(2,1)}, bf16[1024,1152]{1,0:T(8,128)(2,1)}, u32[]{:S(2)}, u32[]{:S(2)}) collective-permute-start(bf16[1024,1152]{1,0:T(8,128)(2,1)} %collective-permute-done), channel_id=1, source_target_pairs={{126,0},{0,2},{2,4},{4,6},{6,8},{8,10},{10,12},{12,14},{14,16},{16... | collective-permute-start | bytes 7077896 | tf_op jit(solution)/shard_map/ppermute | solution.py:12
  234.3 1.1 copy-start
  240.6 88.0 %collective-permute-start.5 = (f32[1024,1152]{1,0:T(8,128)}, f32[1024,1152]{1,0:T(8,128)}, u32[]{:S(2)}, u32[]{:S(2)}) collective-permute-start(f32[1024,1152]{1,0:T(8,128)} %add.239), channel_id=1, source_target_pairs={{126,0},{0,2},{2,4},{4,6},{6,8},{8,10},{10,12},{12,14},{14,16},{16... | collective-permute-start | bytes 14155784 | tf_op jit(solution)/shard_map/ppermute | solution.py:12
  243.1 76.7 %collective-permute-start.2 = (bf16[1024,1152]{1,0:T(8,128)(2,1)}, bf16[1024,1152]{1,0:T(8,128)(2,1)}, u32[]{:S(2)}, u32[]{:S(2)}) collective-permute-start(bf16[1024,1152]{1,0:T(8,128)(2,1)} %collective-permute-done.1), channel_id=1, source_target_pairs={{126,0},{0,2},{2,4},{4,6},{6,8},{8,10},{10,12},{12,14},{14,16},{16... | collective-permute-start | bytes 7077896 | tf_op jit(solution)/shard_map/ppermute | solution.py:12
  327.5 1.1 copy-start.4
  331.6 92.1 %collective-permute-start.6 = (f32[1024,1152]{1,0:T(8,128)S(1)}, f32[1024,1152]{1,0:T(8,128)}, u32[]{:S(2)}, u32[]{:S(2)}) collective-permute-start(f32[1024,1152]{1,0:T(8,128)S(1)} %add.240), channel_id=1, source_target_pairs={{6,0},{8,2},{10,4},{12,6},{14,8},{16,10},{18,12},{20,14},{22,16},{... | collective-permute-start | bytes 14155784 | tf_op jit(solution)/shard_map/ppermute | solution.py:12
  426.7 2.7 copy-start.1
  429.4 2.7 copy-start.5
  439.1 31.5 %copy-start.2 = (s32[512]{0:T(512)S(1)}, s32[512]{0:T(512)}, u32[]{:S(2)}) copy-start(s32[512]{0:T(512)} %param.8) | copy-start | bytes 6148
  439.1 118.3 %all-to-all-start.2 = ((bf16[128,4,1152]{2,1,0:T(4,128)(2,1)}), bf16[128,4,1152]{2,1,0:T(4,128)(2,1)S(1)}, u32[]{:S(2)}, u32[]{:S(2)}) async-start(bf16[128,4,1152]{2,1,0:T(4,128)(2,1)} %select_select_fusion.1), calls=%async_computation.2 | async-start | bytes 2359296 | tf_op jit(solution)/shard_map/all_to_all | solution.py:111
Sparse Core Ops, SparseCore 0:
  423.9 98.4 reduce-scatter.1
where the time goes:
time: 575 us
  waiting for transfers between devices  340 us (59%)
  blocking collectives  77.1 us (13%)
  starting transfers between devices  57.9 us (10%)
  matrix products  37.2 us (6%)
  between operations  28.7 us (5%)
  local copies, waits for them, and re-layouts  17.1 us (3%)
  other arithmetic  16.7 us (3%)
    ppermute x7, waiting for transfers between devices, from_behind(): return lax.ppermute(block, axis, route)  318 us
    psum x1, blocking collectives, local(): lax.psum((loss_total, scale_total, bias_total), ('dp', 'sub'))  77.1 us
    all_to_all x1, starting transfers between devices, local(): lax.all_to_all(returning.reshape(devices, pair_cap, columns), ('dp', 'sub...  31.4 us
    all_to_all x1, waiting for transfers between devices, local(): lax.all_to_all(outgoing.reshape(devices, pair_cap, columns), ('dp', 'sub'...  17.6 us
    dot_general x4, matrix products, pair_terms(): inner = jnp.dot(slot_rows, block_rows.T, preferred_element_type=jnp.float32)  15.3 us
  transfers between devices with their start and end apart: 11, of which 6 were waited for; matrix products, arithmetic and copies ran while one was open for 7% of the time, Pallas kernels for 0%

commit v1 on v0

v1 whole, which is shorter than its diff:
```python
import functools

import jax
import jax.numpy as jnp
from jax import lax
from jax.experimental import pallas as pl
from jax.experimental.pallas import tpu as pltpu
from jax.sharding import PartitionSpec as P

STOPS = 4
LANES = 128
MESH = pl.DeviceIdType.MESH
F32 = jnp.float32
BF16 = jnp.bfloat16


def iota(shape, axis):
    return lax.broadcasted_iota(jnp.int32, shape, axis)


def mm(a, b):
    return lax.dot_general(a, b, (((1,), (0,)), ((), ())), preferred_element_type=F32)


def mm_nt(a, b):
    return lax.dot_general(a, b, (((1,), (1,)), ((), ())), preferred_element_type=F32)


def kernel(
    n_dp,
    pairs,
    scale_ref,
    bias_ref,
    dest_ref,
    labels_ref,
    images_ref,
    text_ref,
    gi_ref,
    gt_ref,
    loss_ref,
    gscale_ref,
    gbias_ref,
    send,
    recv,
    back,
    back_recv,
    home,
    part,
    part_in,
    sl,
    lab,
    wt,
    wn,
    own,
    own_in,
    pre,
    pre_in,
    ret1_out,
    ret1,
    ret2_out,
    ret2,
    ret2b,
    slot_grad,
    text_out,
    text_in,
    p_t,
    q_t,
    stat,
    stat_in,
    a2a_send,
    a2a_recv,
    local_sem,
    ss,
    rs,
):
    rows, columns = images_ref.shape
    texts = text_ref.shape[0]
    slots = labels_ref.shape[1]
    half = slots // 2
    chips = n_dp
    n_m = n_dp // 2
    per_chip = rows // chips
    width = send.shape[2]
    tail = columns - width
    t_tile = min(256, texts // 2)

    d = lax.axis_index("dp")
    s = lax.axis_index("sub")
    m = lax.div(d, 2)
    c = lax.rem(d, 2)
    chip = m * 2 + s
    partner = (m * 2 + (1 - c), s)
    across = (d, 1 - s)

    def chip_dev(i):
        i = lax.rem(i + chips, chips)
        return (lax.div(i, 2) * 2 + c, lax.rem(i, 2))

    def m_dev(step):
        return (lax.rem(m + step + n_m, n_m) * 2 + c, s)

    def dp_dev(step):
        return (lax.rem(d + step + n_dp, n_dp), s)

    barrier = pltpu.get_barrier_semaphore()

    def greet(k, carry):
        pl.semaphore_signal(barrier, inc=1, device_id=chip_dev(chip + k), device_id_type=MESH)
        return carry

    lax.fori_loop(1, chips, greet, 0)
    for dev in (partner, dp_dev(1), dp_dev(3)):
        pl.semaphore_signal(barrier, inc=1, device_id=dev, device_id_type=MESH)

    def remote(src, dst, k, dev):
        return pltpu.make_async_remote_copy(
            src_ref=src,
            dst_ref=dst,
            send_sem=ss.at[k],
            recv_sem=rs.at[k],
            device_id=dev,
            device_id_type=MESH,
        )

    q = dest_ref[...]
    valid = q >= 0
    group = lax.div(jnp.maximum(q, 0), 2 * slots)
    rest = jnp.maximum(q, 0) - group * (2 * slots)
    to_sub = lax.div(rest, slots)
    slot_id = rest - to_sub * slots
    even = (group & 1) == 0
    to_m = lax.div((group + (n_dp - 1)) & (n_dp - 1), 2)
    rel = (to_m * 2 + to_sub - chip + (chips - 1)) & (chips - 1)
    rel = jnp.where(valid, rel, -1)
    onehot = rel == iota((chips, rows), 0)
    earlier = (iota((rows, rows), 0) < iota((rows, rows), 1)).astype(F32).astype(BF16)
    onehot_f = onehot.astype(F32)
    rank = mm(onehot_f.astype(BF16), earlier)
    within = jnp.sum(onehot_f * rank, axis=0, keepdims=True)
    placed = jnp.where(valid, rel.astype(F32) * float(per_chip) + within, -1.0)
    placed_col = jnp.transpose(jnp.broadcast_to(placed, (LANES, rows)))[:, :1].astype(jnp.int32)
    p_t[...] = (placed_col == iota((rows, rows), 1)).astype(F32).astype(BF16)
    placed_int = placed.astype(jnp.int32)
    id_plus = (slot_id + 1).astype(F32)
    id_odd = jnp.where(valid & jnp.logical_not(even), id_plus, 0.0)
    id_even = jnp.where(valid & even, id_plus, 0.0)
    which = iota((LANES, rows), 0)
    id_rows = jnp.where(which == 0, id_odd, jnp.where(which == 1, id_even, 0.0))
    ids_block = jnp.transpose(id_rows).astype(BF16)
    row_tile = min(128, rows)
    for r in range(rows // row_tile):
        p_mat = (placed_int == iota((row_tile, rows), 0) + r * row_tile).astype(F32).astype(BF16)
        n = row_tile // per_chip
        first = mm(p_mat, images_ref[:, :width]).reshape(n, per_chip, width)
        second = mm(p_mat, images_ref[:, width:]).reshape(n, per_chip, tail)
        third = mm(p_mat, ids_block).reshape(n, per_chip, LANES)
        second = jnp.concatenate([second, third], axis=2)
        send[r * n : (r + 1) * n] = jnp.concatenate([first, second], axis=1).astype(BF16)

    pl.semaphore_wait(barrier, chips - 1 + 3)

    lab_copies = [
        remote(labels_ref, lab.at[slot], 9 + step, dp_dev(-step))
        for step, slot in ((1, 1 - c), (2, 1 + c), (3, 3 - c))
    ]
    for copy in lab_copies:
        copy.start()
    lab_own = pltpu.make_async_copy(labels_ref, lab.at[3 - 3 * c], local_sem.at[0])
    lab_own.start()

    def all_start(buf, into, which_sem, sign):
        def step(k, carry):
            pltpu.make_async_remote_copy(
                src_ref=buf.at[k],
                dst_ref=into.at[k],
                send_sem=a2a_send.at[which_sem],
                recv_sem=a2a_recv.at[which_sem],
                device_id=chip_dev(chip + sign * (k + 1)),
                device_id_type=MESH,
            ).start()
            return carry

        lax.fori_loop(0, chips - 1, step, 0)
        own_copy = pltpu.make_async_copy(
            buf.at[chips - 1], into.at[chips - 1], local_sem.at[1 + which_sem]
        )
        own_copy.start()
        return own_copy

    def all_desc(buf, into, which_sem):
        return pltpu.make_async_remote_copy(
            src_ref=buf.at[pl.ds(0, chips - 1)],
            dst_ref=into.at[pl.ds(0, chips - 1)],
            send_sem=a2a_send.at[which_sem],
            recv_sem=a2a_recv.at[which_sem],
            device_id=partner,
            device_id_type=MESH,
        )

    out_own = all_start(send, recv, 0, 1)
    out_all = all_desc(send, recv, 0)
    out_own.wait()
    out_all.wait_recv()

    ids = recv[:, per_chip:, tail:].astype(F32).reshape(rows, LANES).astype(jnp.int32)
    lane = iota((rows, 2 * slots), 1)
    filled = jnp.where(lane < slots, ids[:, :1], ids[:, 1:2] + slots)
    q_t[...] = (filled == lane + 1).astype(F32).astype(BF16)
    ids_t = jnp.transpose(ids.astype(F32)).astype(jnp.int32)
    first = recv[:, :per_chip, :].astype(F32).reshape(rows, width).astype(BF16)
    second = recv[:, per_chip:, :tail].astype(F32).reshape(rows, tail).astype(BF16)
    part_copies = []
    for g in range(2):
        q_mat = (ids_t[g : g + 1, :] == iota((slots, rows), 0) + 1).astype(F32).astype(BF16)
        here = pl.ds(g * slots, slots)
        part[here, :width] = mm(q_mat, first).astype(BF16)
        part[here, width:] = mm(q_mat, second).astype(BF16)
        copy = remote(part.at[here], part_in.at[here], g, partner)
        copy.start()
        part_copies.append(copy)
    lab_own.wait()
    for copy in lab_copies:
        copy.wait()
    for g in range(2):
        part_copies[g].wait()
        here = pl.ds(g * slots, slots)
        home[here, :] = (part[here, :].astype(F32) + part_in[here, :].astype(F32)).astype(BF16)
    half_c = pl.ds(pl.multiple_of(c * half, half), half)
    half_o = pl.ds(pl.multiple_of((1 - c) * half, half), half)

    def ext1(which_half):
        return sl.at[0, which_half]

    ext1_copy = remote(home.at[half_c], ext1(half_c), 2, m_dev(-1))
    ext1_copy.start()
    ext2_copy = remote(home.at[pl.ds(slots, slots)], sl.at[1], 3, m_dev(1 - 2 * c))
    ext2_copy.start()

    factor = scale_ref[0]
    offset = bias_ref[0]

    def slot_rows(o):
        if o < 2:
            return home[o * slots : (o + 1) * slots, :]
        return sl[o - 2]

    def group_terms(o, sums):
        labels = lab[o]

        def chunk(j, sums):
            at = pl.multiple_of(j * t_tile, t_tile)
            inner = mm_nt(text_ref[pl.ds(at, t_tile), :], slot_rows(o))
            logits = factor * inner + offset
            e = jnp.exp(-jnp.abs(logits))
            u = 1.0 + e
            r = 1.0 / u
            log1p = jnp.log(u) + (e - (u - 1.0)) * r
            positive = labels == iota((t_tile, slots), 0) + (d * texts + at)
            sig = jnp.where(logits >= 0.0, r, e * r)
            grad = jnp.where(positive, sig - 1.0, sig)
            loss = jnp.maximum(logits, 0.0) + log1p - jnp.where(positive, logits, 0.0)
            weights = grad.astype(BF16)
            wt[pl.ds(at, t_tile), o * slots : (o + 1) * slots] = weights
            wn[:, pl.ds(at, t_tile)] = jnp.transpose(weights)
            return (
                sums[0] + jnp.sum(loss, axis=0, keepdims=True),
                sums[1] + jnp.sum(grad * inner, axis=0, keepdims=True),
                sums[2] + jnp.sum(grad, axis=0, keepdims=True),
            )

        return lax.fori_loop(0, texts // t_tile, chunk, sums)

    c_tile = 384 if columns % 384 == 0 else LANES

    def image_term(out, base, cast=None):
        def tile(j, carry):
            at = pl.ds(pl.multiple_of(j * c_tile, c_tile), c_tile)
            res = mm(wn[...], text_ref[:, at])
            out[base : base + slots, at] = res if cast is None else res.astype(cast)
            return carry

        lax.fori_loop(0, columns // c_tile, tile, 0)

    sums = (jnp.zeros((1, slots), F32),) * 3
    sums = group_terms(0, sums)
    image_term(own, 0)
    sums = group_terms(1, sums)
    image_term(own, slots)
    own_copy = remote(own, own_in, 4, partner)
    own_copy.start()

    ext1_copy.wait_recv()
    ext1_fwd = remote(ext1(half_c), ext1(half_c), 5, partner)
    ext1_fwd.start()
    ext1_fwd.wait_recv()
    sums = group_terms(2, sums)
    image_term(pre, 0)
    pre_copy = remote(pre.at[half_o], pre_in, 6, partner)
    pre_copy.start()

    ext2_copy.wait_recv()
    sums = group_terms(3, sums)
    image_term(ret2_out, 0, BF16)
    ret2_copy = remote(ret2_out, ret2, 7, m_dev(2 * c - 1))
    ret2_copy.start()

    pre_copy.wait_recv()
    ret1_out[...] = (pre[half_c, :] + pre_in[...]).astype(BF16)
    ret1_copy = remote(ret1_out, ret1.at[half_c], 8, m_dev(1))
    ret1_copy.start()

    lane = iota((8, LANES), 1)
    totals = [jnp.sum(x, axis=1, keepdims=True) for x in sums]
    kind = lax.rem(lane, 3)
    stat[...] = jnp.where(kind == 0, totals[0], jnp.where(kind == 1, totals[1], totals[2]))
    stat_copy = remote(stat, stat_in, 9, partner)
    stat_copy.start()

    n_text = (texts // 2) // t_tile
    text_copies = []

    def text_term(at):
        at = pl.ds(pl.multiple_of(at, t_tile), t_tile)
        res = mm(wt[at, : 2 * slots], home[...])
        res += mm(wt[at, 2 * slots : 3 * slots], sl[0])
        return res + mm(wt[at, 3 * slots :], sl[1])

    for j in range(n_text):
        rows_j = pl.ds(j * t_tile, t_tile)
        text_out[rows_j, :] = text_term((1 - s) * (texts // 2) + j * t_tile).astype(BF16)
        copy = remote(text_out.at[rows_j], text_in.at[rows_j], 15 + j, across)
        copy.start()
        text_copies.append(copy)

    for j in range(n_text):
        gt_ref[j * t_tile : (j + 1) * t_tile, :] = text_term(s * (texts // 2) + j * t_tile)

    ret1_copy.wait_recv()
    ret1_fwd = remote(ret1.at[half_c], ret1.at[half_c], 13, partner)
    ret1_fwd.start()
    ret2_copy.wait_recv()
    ret2_fwd = remote(ret2, ret2b, 14, partner)
    ret2_fwd.start()
    own_copy.wait_recv()
    stat_copy.wait_recv()

    value = stat[...] + stat_in[...]
    top = value.astype(BF16).astype(F32)
    middle = (value - top).astype(BF16).astype(F32)
    low = value - top - middle
    payload = jnp.where(lane < 3, top, jnp.where(lane < 6, middle, jnp.where(lane < 9, low, 0.0)))

    ret1_fwd.wait_recv()
    odd = own[:slots, :] + own_in[:slots, :] + ret1[...].astype(F32)
    slot_grad[:slots, :] = (factor * odd).astype(BF16)
    ret2_fwd.wait_recv()
    evn = own[slots:, :] + own_in[slots:, :] + (ret2[...].astype(F32) + ret2b[...].astype(F32))
    slot_grad[slots:, :] = (factor * evn).astype(BF16)

    payload_rows = jnp.broadcast_to(payload[:per_chip][None], (row_tile // per_chip, per_chip, LANES))
    for r in range(rows // row_tile):
        n = row_tile // per_chip
        q_rows = q_t[r * row_tile : (r + 1) * row_tile, :]
        first = mm(q_rows, slot_grad[:, :width]).reshape(n, per_chip, width)
        second = mm(q_rows, slot_grad[:, width:]).reshape(n, per_chip, tail)
        second = jnp.concatenate([second, payload_rows], axis=2)
        back[r * n : (r + 1) * n] = jnp.concatenate([first, second], axis=1).astype(BF16)

    back_own = all_start(back, back_recv, 1, -1)
    back_all = all_desc(back, back_recv, 1)
    for j in range(n_text):
        text_copies[j].wait_recv()
        rows_j = pl.ds(j * t_tile, t_tile)
        gt_ref[rows_j, :] = factor * (gt_ref[rows_j, :] + text_in[rows_j, :].astype(F32))
    back_own.wait()
    back_all.wait_recv()

    first = back_recv[:, :per_chip, :].astype(F32).reshape(rows, width).astype(BF16)
    second = back_recv[:, per_chip:, :tail].astype(F32).reshape(rows, tail).astype(BF16)
    for r in range(rows // row_tile):
        at = slice(r * row_tile, (r + 1) * row_tile)
        p_rows = p_t[at, :]
        gi_ref[at, :width] = mm(p_rows, first).astype(BF16)
        gi_ref[at, width:] = mm(p_rows, second).astype(BF16)

    sums_in = back_recv[:, per_chip:, tail:].astype(F32)[:, 0, :].astype(BF16)
    source = (chip + 1 + iota((chips, chips), 1)) & (chips - 1)
    order = (source == iota((chips, chips), 0)).astype(F32).astype(BF16)
    total = jnp.sum(mm(order, sums_in), axis=0, keepdims=True)
    lane = iota((1, LANES), 1)
    for k, ref in enumerate((loss_ref, gscale_ref, gbias_ref)):
        picked = (lane < 9) & (lax.rem(lane, 3) == k)
        ref[0] = jnp.sum(jnp.where(picked, total, 0.0)) / pairs

    out_all.wait_send()
    back_all.wait_send()
    for copy in (
        ext1_copy,
        ext2_copy,
        own_copy,
        ext1_fwd,
        pre_copy,
        ret2_copy,
        ret1_copy,
        stat_copy,
        ret1_fwd,
        ret2_fwd,
        *text_copies,
    ):
        copy.wait_send()


def local(images, text_embeds, dest_slot, labels, logit_scale, logit_bias):
    n_dp = lax.axis_size("dp")
    rows, columns = images.shape
    texts = text_embeds.shape[0]
    slots = labels.shape[0]
    chips = n_dp
    per_chip = rows // chips
    width = (columns + LANES) // 2
    pairs = float(slots * n_dp * 2 * STOPS * texts)
    vmem = pl.BlockSpec(memory_space=pltpu.VMEM)
    smem = pl.BlockSpec(memory_space=pltpu.SMEM)
    message = pltpu.VMEM((chips, 2 * per_chip, width), BF16)

    def buf(n, dtype=BF16):
        return pltpu.VMEM((n, columns), dtype)

    scalar = jax.ShapeDtypeStruct((1,), F32)
    return pl.pallas_call(
        functools.partial(kernel, n_dp, pairs),
        out_shape=(
            jax.ShapeDtypeStruct((rows, columns), BF16),
            jax.ShapeDtypeStruct((texts // 2, columns), F32),
            scalar,
            scalar,
            scalar,
        ),
        in_specs=[smem, smem, vmem, vmem, vmem, vmem],
        out_specs=(vmem, vmem, smem, smem, smem),
        scratch_shapes=[
            message,
            message,
            message,
            message,
            buf(2 * slots),
            buf(2 * slots),
            buf(2 * slots),
            pltpu.VMEM((2, slots, columns), BF16),
            pltpu.VMEM((4, 1, slots), jnp.int32),
            pltpu.VMEM((texts, 4 * slots), BF16),
            pltpu.VMEM((slots, texts), BF16),
            buf(2 * slots, F32),
            buf(2 * slots, F32),
            buf(slots, F32),
            buf(slots // 2, F32),
            buf(slots // 2),
            buf(slots),
            buf(slots),
            buf(slots),
            buf(slots),
            buf(2 * slots),
            buf(texts // 2),
            buf(texts // 2),
            pltpu.VMEM((rows, rows), BF16),
            pltpu.VMEM((rows, 2 * slots), BF16),
            pltpu.VMEM((8, LANES), F32),
            pltpu.VMEM((8, LANES), F32),
            pltpu.SemaphoreType.DMA((2,)),
            pltpu.SemaphoreType.DMA((2,)),
            pltpu.SemaphoreType.DMA((3,)),
            pltpu.SemaphoreType.DMA((24,)),
            pltpu.SemaphoreType.DMA((24,)),
        ],
        compiler_params=pltpu.CompilerParams(
            collective_id=0,
            has_side_effects=True,
            vmem_limit_bytes=58 * 1024 * 1024,
        ),
    )(
        logit_scale,
        logit_bias,
        dest_slot.reshape(1, rows),
        labels.reshape(1, slots),
        images,
        text_embeds,
    )


def solution(mesh):
    return jax.shard_map(
        local,
        mesh=mesh,
        in_specs=(
            P(("dp", "sub"), None),
            P("dp", None),
            P(("dp", "sub")),
            P(("dp", "sub")),
            P(),
            P(),
        ),
        out_specs=(P(("dp", "sub"), None), P(("dp", "sub"), None), P(), P(), P()),
        check_vma=False,
    )
```

time: 575 us -> 130 us (0.23)
  waiting for transfers between devices: 340 us -> 0 us
  Pallas kernels: 0 us -> 118 us
  blocking collectives: 77.1 us -> 0 us
  starting transfers between devices: 57.9 us -> 0 us
  matrix products: 37.2 us -> 0 us
  between operations: 28.7 us -> 7.12 us
  other arithmetic: 16.7 us -> 0 us
  local copies, waits for them, and re-layouts: 17.1 us -> 3.93 us
    ppermute x7 -> x0, waiting for transfers between devices: 318 us -> none  [from_behind(): return lax.ppermute(block, axis, route)]
    pallas_call x0 -> x1, Pallas kernels: none -> 118 us  [local(): pl.pallas_call(functools.partial(kernel, n_dp, pairs), out_shape=(jax.Sha...]
    psum x1 -> x0, blocking collectives: 77.1 us -> none  [local(): lax.psum((loss_total, scale_total, bias_total), ('dp', 'sub'))]
    all_to_all x3 -> x0, starting transfers between devices: 48.1 us -> none  [the longest x1 31.4 us: local(): lax.all_to_all(returning.reshape(devices, pair_cap, columns), ('dp', 'sub...]
    dot_general x12 -> x0, matrix products: 37.2 us -> none  [the longest x4 15.3 us: pair_terms(): inner = jnp.dot(slot_rows, block_rows.T, preferred_element_type=jnp.float32)]
    all_to_all x3 -> x0, waiting for transfers between devices: 22.2 us -> none  [the longest x1 17.6 us: local(): lax.all_to_all(outgoing.reshape(devices, pair_cap, columns), ('dp', 'sub'...]
    ppermute x7 -> x0, starting transfers between devices: 9.77 us -> none  [from_behind(): return lax.ppermute(block, axis, route)]
    scatter x3 -> x0, local copies, waits for them, and re-layouts: 9.04 us -> none  [the longest x1 3.79 us: local(): jnp.zeros((devices * pair_cap, columns), jnp.bfloat16).at[placed]]
  transfers between devices with their start and end apart: 11 -> 0, of which waited for: 6 -> 0; matrix products, arithmetic and copies ran while one was open for 7% -> 0% of each run, Pallas kernels for 0% -> 0%
where the time goes in v1:
time: 130 us; the launch traced here: 129 us
  Pallas kernels  118 us (91%)
  between operations  7.12 us (5%)
  local copies, waits for them, and re-layouts  3.93 us (3%)
    pallas_call x1, Pallas kernels, local(): pl.pallas_call(functools.partial(kernel, n_dp, pairs), out_shape=(jax.Sha...  118 us
    unnamed x4, local copies, waits for them, and re-layouts  3.93 us

profile of v1, /device:TPU:1, one launch (start us, length us, event | category | flops | bytes accessed | tf_op | source)
XLA Modules:
  0.0 129.4 jit_solution(17998343978474378959)
XLA Ops:
  1.9 118.4 %shard_map.101 = (bf16[512,1152]{1,0:T(8,128)(2,1)}, f32[512,1152]{1,0:T(8,128)}, f32[1]{0:T(128)}, f32[1]{0:T(128)}, f32[1]{0:T(128)}) custom-call(f32[1]{0:T(128)S(6)} %copy.16.scale_ref, f32[1]{0:T(128)S(6)} %copy.17.bias_ref, s32[1,512]{1,0:T(1,128)} %bitcast.2, s32[1,256]{1,0:T(1,128)} %bitcast.3, bf16[512,1152]{1,0:T(8,128)(2,1)} %images_ref.1, ...), custom_call_target="tpu_custom_call" | custom-call | tf_op jit(solution)/shard_map/pallas_call | solution.py:430
  120.3 0.0 copy-start
  120.3 2.5 %copy.18 = bf16[512,1152]{1,0:T(8,128)(2,1)} copy(bf16[512,1152]{1,0:T(8,128)(2,1)} %get-tuple-element.10) | data formatting | bytes 2359296
  122.8 0.0 copy-done
  122.8 1.4 %copy.19 = f32[512,1152]{1,0:T(8,128)} copy(f32[512,1152]{1,0:T(8,128)S(1)} %copy-done) | data formatting | bytes 4718592
Async XLA Ops:
  120.3 2.5 %copy-start = (f32[512,1152]{1,0:T(8,128)S(1)}, f32[512,1152]{1,0:T(8,128)}, u32[]{:S(2)}) copy-start(f32[512,1152]{1,0:T(8,128)} %get-tuple-element.11) | copy-start | bytes 7077892

commit v2 on v1

--- a/solution.py
+++ b/solution.py
@@ -28,22 +28,20 @@
 
 def kernel(
     n_dp,
-    pairs,
     scale_ref,
     bias_ref,
     dest_ref,
     labels_ref,
     images_ref,
+    text_hbm,
+    back_recv,
+    text_in,
+    gt_hbm,
+    p_hbm,
     text_ref,
-    gi_ref,
-    gt_ref,
-    loss_ref,
-    gscale_ref,
-    gbias_ref,
     send,
     recv,
     back,
-    back_recv,
     home,
     part,
     part_in,
@@ -61,8 +59,9 @@
     ret2,
     ret2b,
     slot_grad,
+    text_sum,
     text_out,
-    text_in,
+    gt,
     p_t,
     q_t,
     stat,
@@ -75,6 +74,7 @@
 ):
     rows, columns = images_ref.shape
     texts = text_ref.shape[0]
+    text_half = texts // 2
     slots = labels_ref.shape[1]
     half = slots // 2
     chips = n_dp
@@ -101,6 +101,9 @@
 
     def dp_dev(step):
         return (lax.rem(d + step + n_dp, n_dp), s)
+
+    text_copy = pltpu.make_async_copy(text_hbm, text_ref, local_sem.at[3])
+    text_copy.start()
 
     barrier = pltpu.get_barrier_semaphore()
 
@@ -140,6 +143,8 @@
     placed = jnp.where(valid, rel.astype(F32) * float(per_chip) + within, -1.0)
     placed_col = jnp.transpose(jnp.broadcast_to(placed, (LANES, rows)))[:, :1].astype(jnp.int32)
     p_t[...] = (placed_col == iota((rows, rows), 1)).astype(F32).astype(BF16)
+    p_copy = pltpu.make_async_copy(p_t, p_hbm, local_sem.at[4])
+    p_copy.start()
     placed_int = placed.astype(jnp.int32)
     id_plus = (slot_id + 1).astype(F32)
     id_odd = jnp.where(valid & jnp.logical_not(even), id_plus, 0.0)
@@ -168,7 +173,7 @@
     lab_own = pltpu.make_async_copy(labels_ref, lab.at[3 - 3 * c], local_sem.at[0])
     lab_own.start()
 
-    def all_start(buf, into, which_sem, sign):
+    def all_start(buf, into, which_sem, sign, lo, hi):
         def step(k, carry):
             pltpu.make_async_remote_copy(
                 src_ref=buf.at[k],
@@ -180,12 +185,14 @@
             ).start()
             return carry
 
-        lax.fori_loop(0, chips - 1, step, 0)
-        own_copy = pltpu.make_async_copy(
+        lax.fori_loop(lo, min(hi, chips - 1), step, 0)
+
+    def own_start(buf, into, which_sem):
+        copy = pltpu.make_async_copy(
             buf.at[chips - 1], into.at[chips - 1], local_sem.at[1 + which_sem]
         )
-        own_copy.start()
-        return own_copy
+        copy.start()
+        return copy
 
     def all_desc(buf, into, which_sem):
         return pltpu.make_async_remote_copy(
@@ -197,7 +204,8 @@
             device_id_type=MESH,
         )
 
-    out_own = all_start(send, recv, 0, 1)
+    all_start(send, recv, 0, 1, 0, chips)
+    out_own = own_start(send, recv, 0)
     out_all = all_desc(send, recv, 0)
     out_own.wait()
     out_all.wait_recv()
@@ -234,10 +242,15 @@
     ext1_copy = remote(home.at[half_c], ext1(half_c), 2, m_dev(-1))
     ext1_copy.start()
     ext2_copy = remote(home.at[pl.ds(slots, slots)], sl.at[1], 3, m_dev(1 - 2 * c))
-    ext2_copy.start()
-
-    factor = scale_ref[0]
-    offset = bias_ref[0]
+
+    @pl.when(c == 0)
+    def _():
+        ext2_copy.start()
+
+    text_copy.wait()
+
+    factor = scale_ref[...]
+    offset = bias_ref[...]
 
     def slot_rows(o):
         if o < 2:
@@ -261,7 +274,7 @@
             loss = jnp.maximum(logits, 0.0) + log1p - jnp.where(positive, logits, 0.0)
             weights = grad.astype(BF16)
             wt[pl.ds(at, t_tile), o * slots : (o + 1) * slots] = weights
-            wn[:, pl.ds(at, t_tile)] = jnp.transpose(weights)
+            wn[o, :, pl.ds(at, t_tile)] = jnp.transpose(weights)
             return (
                 sums[0] + jnp.sum(loss, axis=0, keepdims=True),
                 sums[1] + jnp.sum(grad * inner, axis=0, keepdims=True),
@@ -272,42 +285,79 @@
 
     c_tile = 384 if columns % 384 == 0 else LANES
 
-    def image_term(out, base, cast=None):
+    def image_term(out, base, o, cast=None):
         def tile(j, carry):
             at = pl.ds(pl.multiple_of(j * c_tile, c_tile), c_tile)
-            res = mm(wn[...], text_ref[:, at])
+            res = mm(wn[o], text_ref[:, at])
             out[base : base + slots, at] = res if cast is None else res.astype(cast)
             return carry
 
         lax.fori_loop(0, columns // c_tile, tile, 0)
 
+    n_text = text_half // t_tile
+
+    def text_rows(base, j):
+        return pl.ds(pl.multiple_of(base + j * t_tile, t_tile), t_tile)
+
+    def text_part(base, j, first, last, rows_of):
+        return mm(wt[text_rows(base, j), first * slots : last * slots], rows_of())
+
+    mine, theirs = s * text_half, (1 - s) * text_half
+
     sums = (jnp.zeros((1, slots), F32),) * 3
     sums = group_terms(0, sums)
-    image_term(own, 0)
     sums = group_terms(1, sums)
-    image_term(own, slots)
+
+    @pl.when(c == 1)
+    def _():
+        ext2_copy.start()
+
+    image_term(own, 0, 0)
+    image_term(own, slots, 1)
     own_copy = remote(own, own_in, 4, partner)
     own_copy.start()
+    for j in range(n_text):
+        here = pl.ds(j * t_tile, t_tile)
+        text_sum[here, :] = text_part(theirs, j, 0, 2, lambda: home[...])
 
     ext1_copy.wait_recv()
     ext1_fwd = remote(ext1(half_c), ext1(half_c), 5, partner)
     ext1_fwd.start()
+    for j in range(n_text):
+        here = pl.ds(j * t_tile, t_tile)
+        gt[here, :] = text_part(mine, j, 0, 2, lambda: home[...])
     ext1_fwd.wait_recv()
     sums = group_terms(2, sums)
-    image_term(pre, 0)
+    image_term(pre, 0, 2)
     pre_copy = remote(pre.at[half_o], pre_in, 6, partner)
     pre_copy.start()
-
-    ext2_copy.wait_recv()
-    sums = group_terms(3, sums)
-    image_term(ret2_out, 0, BF16)
-    ret2_copy = remote(ret2_out, ret2, 7, m_dev(2 * c - 1))
-    ret2_copy.start()
-
+    for j in range(n_text):
+        here = pl.ds(j * t_tile, t_tile)
+        text_sum[here, :] += text_part(theirs, j, 2, 3, lambda: sl[0])
     pre_copy.wait_recv()
     ret1_out[...] = (pre[half_c, :] + pre_in[...]).astype(BF16)
     ret1_copy = remote(ret1_out, ret1.at[half_c], 8, m_dev(1))
     ret1_copy.start()
+
+    ext2_copy.wait_recv()
+    sums = group_terms(3, sums)
+    text_copies = []
+
+    def send_text(j):
+        here = pl.ds(j * t_tile, t_tile)
+        text_out[here, :] = (
+            text_sum[here, :] + text_part(theirs, j, 3, 4, lambda: sl[1])
+        ).astype(BF16)
+        copy = remote(text_out.at[here], text_in.at[here], 15 + j, across)
+        copy.start()
+        text_copies.append(copy)
+
+    send_text(0)
+    image_term(ret2_out, 0, 3, BF16)
+    ret2_copy = remote(ret2_out, ret2, 7, m_dev(2 * c - 1))
+    ret2_copy.start()
+    for j in range(1, n_text):
+        send_text(j)
 
     lane = iota((8, LANES), 1)
     totals = [jnp.sum(x, axis=1, keepdims=True) for x in sums]
@@ -316,24 +366,13 @@
     stat_copy = remote(stat, stat_in, 9, partner)
     stat_copy.start()
 
-    n_text = (texts // 2) // t_tile
-    text_copies = []
-
-    def text_term(at):
-        at = pl.ds(pl.multiple_of(at, t_tile), t_tile)
-        res = mm(wt[at, : 2 * slots], home[...])
-        res += mm(wt[at, 2 * slots : 3 * slots], sl[0])
-        return res + mm(wt[at, 3 * slots :], sl[1])
-
     for j in range(n_text):
-        rows_j = pl.ds(j * t_tile, t_tile)
-        text_out[rows_j, :] = text_term((1 - s) * (texts // 2) + j * t_tile).astype(BF16)
-        copy = remote(text_out.at[rows_j], text_in.at[rows_j], 15 + j, across)
-        copy.start()
-        text_copies.append(copy)
-
-    for j in range(n_text):
-        gt_ref[j * t_tile : (j + 1) * t_tile, :] = text_term(s * (texts // 2) + j * t_tile)
+        here = pl.ds(j * t_tile, t_tile)
+        gt[here, :] += text_part(mine, j, 2, 3, lambda: sl[0]) + text_part(
+            mine, j, 3, 4, lambda: sl[1]
+        )
+    gt_copy = pltpu.make_async_copy(gt, gt_hbm, local_sem.at[5])
+    gt_copy.start()
 
     ret1_copy.wait_recv()
     ret1_fwd = remote(ret1.at[half_c], ret1.at[half_c], 13, partner)
@@ -365,32 +404,16 @@
         second = mm(q_rows, slot_grad[:, width:]).reshape(n, per_chip, tail)
         second = jnp.concatenate([second, payload_rows], axis=2)
         back[r * n : (r + 1) * n] = jnp.concatenate([first, second], axis=1).astype(BF16)
-
-    back_own = all_start(back, back_recv, 1, -1)
+        all_start(back, back_recv, 1, -1, r * n, (r + 1) * n)
+
+    back_own = own_start(back, back_recv, 1)
     back_all = all_desc(back, back_recv, 1)
-    for j in range(n_text):
-        text_copies[j].wait_recv()
-        rows_j = pl.ds(j * t_tile, t_tile)
-        gt_ref[rows_j, :] = factor * (gt_ref[rows_j, :] + text_in[rows_j, :].astype(F32))
+    for copy in text_copies:
+        copy.wait_recv()
+    p_copy.wait()
+    gt_copy.wait()
     back_own.wait()
     back_all.wait_recv()
-
-    first = back_recv[:, :per_chip, :].astype(F32).reshape(rows, width).astype(BF16)
-    second = back_recv[:, per_chip:, :tail].astype(F32).reshape(rows, tail).astype(BF16)
-    for r in range(rows // row_tile):
-        at = slice(r * row_tile, (r + 1) * row_tile)
-        p_rows = p_t[at, :]
-        gi_ref[at, :width] = mm(p_rows, first).astype(BF16)
-        gi_ref[at, width:] = mm(p_rows, second).astype(BF16)
-
-    sums_in = back_recv[:, per_chip:, tail:].astype(F32)[:, 0, :].astype(BF16)
-    source = (chip + 1 + iota((chips, chips), 1)) & (chips - 1)
-    order = (source == iota((chips, chips), 0)).astype(F32).astype(BF16)
-    total = jnp.sum(mm(order, sums_in), axis=0, keepdims=True)
-    lane = iota((1, LANES), 1)
-    for k, ref in enumerate((loss_ref, gscale_ref, gbias_ref)):
-        picked = (lane < 9) & (lax.rem(lane, 3) == k)
-        ref[0] = jnp.sum(jnp.where(picked, total, 0.0)) / pairs
 
     out_all.wait_send()
     back_all.wait_send()
@@ -410,6 +433,34 @@
         copy.wait_send()
 
 
+def finish(n_dp, pairs, per_chip, scale_ref, back_ref, text_in_ref, gt_in_ref, p_ref, *rest):
+    gi_ref, gt_ref, loss_ref, gscale_ref, gbias_ref, rows_in = rest
+    chips, _, width = back_ref.shape
+    rows, columns = rows_in.shape
+    tail = columns - width
+
+    @pl.when(pl.program_id(0) == 0)
+    def _():
+        rows_in[:, :width] = (
+            back_ref[:, :per_chip, :].astype(F32).reshape(rows, width).astype(BF16)
+        )
+        rows_in[:, width:] = (
+            back_ref[:, per_chip:, :tail].astype(F32).reshape(rows, tail).astype(BF16)
+        )
+        chip = lax.div(lax.axis_index("dp"), 2) * 2 + lax.axis_index("sub")
+        sums_in = back_ref[:, per_chip:, tail:].astype(F32)[:, 0, :].astype(BF16)
+        source = (chip + 1 + iota((chips, chips), 1)) & (chips - 1)
+        order = (source == iota((chips, chips), 0)).astype(F32).astype(BF16)
+        total = jnp.sum(mm(order, sums_in), axis=0, keepdims=True)
+        lane = iota((1, LANES), 1)
+        for k, ref in enumerate((loss_ref, gscale_ref, gbias_ref)):
+            picked = (lane < 9) & (lax.rem(lane, 3) == k)
+            ref[0] = jnp.sum(jnp.where(picked, total, 0.0)) / pairs
+
+    gi_ref[...] = mm(p_ref[...], rows_in[...]).astype(BF16)
+    gt_ref[...] = scale_ref[...] * (gt_in_ref[...] + text_in_ref[...].astype(F32))
+
+
 def local(images, text_embeds, dest_slot, labels, logit_scale, logit_bias):
     n_dp = lax.axis_size("dp")
     rows, columns = images.shape
@@ -421,25 +472,25 @@
     pairs = float(slots * n_dp * 2 * STOPS * texts)
     vmem = pl.BlockSpec(memory_space=pltpu.VMEM)
     smem = pl.BlockSpec(memory_space=pltpu.SMEM)
+    hbm = pl.BlockSpec(memory_space=pl.ANY)
     message = pltpu.VMEM((chips, 2 * per_chip, width), BF16)
 
     def buf(n, dtype=BF16):
         return pltpu.VMEM((n, columns), dtype)
 
-    scalar = jax.ShapeDtypeStruct((1,), F32)
-    return pl.pallas_call(
-        functools.partial(kernel, n_dp, pairs),
+    scale = logit_scale.reshape(1, 1)
+    back, text_in, gt, p_t = pl.pallas_call(
+        functools.partial(kernel, n_dp),
         out_shape=(
-            jax.ShapeDtypeStruct((rows, columns), BF16),
+            jax.ShapeDtypeStruct((chips, 2 * per_chip, width), BF16),
+            jax.ShapeDtypeStruct((texts // 2, columns), BF16),
             jax.ShapeDtypeStruct((texts // 2, columns), F32),
-            scalar,
-            scalar,
-            scalar,
+            jax.ShapeDtypeStruct((rows, rows), BF16),
         ),
-        in_specs=[smem, smem, vmem, vmem, vmem, vmem],
-        out_specs=(vmem, vmem, smem, smem, smem),
+        in_specs=[vmem, vmem, vmem, vmem, vmem, hbm],
+        out_specs=(hbm, hbm, hbm, hbm),
         scratch_shapes=[
-            message,
+            buf(texts),
             message,
             message,
             message,
@@ -449,7 +500,7 @@
             pltpu.VMEM((2, slots, columns), BF16),
             pltpu.VMEM((4, 1, slots), jnp.int32),
             pltpu.VMEM((texts, 4 * slots), BF16),
-            pltpu.VMEM((slots, texts), BF16),
+            pltpu.VMEM((4, slots, texts), BF16),
             buf(2 * slots, F32),
             buf(2 * slots, F32),
             buf(slots, F32),
@@ -460,15 +511,16 @@
             buf(slots),
             buf(slots),
             buf(2 * slots),
+            buf(texts // 2, F32),
             buf(texts // 2),
-            buf(texts // 2),
+            buf(texts // 2, F32),
             pltpu.VMEM((rows, rows), BF16),
             pltpu.VMEM((rows, 2 * slots), BF16),
             pltpu.VMEM((8, LANES), F32),
             pltpu.VMEM((8, LANES), F32),
             pltpu.SemaphoreType.DMA((2,)),
             pltpu.SemaphoreType.DMA((2,)),
-            pltpu.SemaphoreType.DMA((3,)),
+            pltpu.SemaphoreType.DMA((6,)),
             pltpu.SemaphoreType.DMA((24,)),
             pltpu.SemaphoreType.DMA((24,)),
         ],
@@ -478,13 +530,38 @@
             vmem_limit_bytes=58 * 1024 * 1024,
         ),
     )(
-        logit_scale,
-        logit_bias,
+        scale,
+        logit_bias.reshape(1, 1),
         dest_slot.reshape(1, rows),
         labels.reshape(1, slots),
         images,
         text_embeds,
     )
+    tiles = 4
+    tile_rows = pl.BlockSpec((rows // tiles, columns), lambda i: (i, 0))
+    tile_texts = pl.BlockSpec((texts // 2 // tiles, columns), lambda i: (i, 0))
+    scalar = jax.ShapeDtypeStruct((1,), F32)
+    return pl.pallas_call(
+        functools.partial(finish, n_dp, pairs, per_chip),
+        out_shape=(
+            jax.ShapeDtypeStruct((rows, columns), BF16),
+            jax.ShapeDtypeStruct((texts // 2, columns), F32),
+            scalar,
+            scalar,
+            scalar,
+        ),
+        grid=(tiles,),
+        in_specs=[
+            pl.BlockSpec((1, 1), lambda i: (0, 0)),
+            pl.BlockSpec(back.shape, lambda i: (0, 0, 0)),
+            tile_texts,
+            tile_texts,
+            pl.BlockSpec((rows // tiles, rows), lambda i: (i, 0)),
+        ],
+        out_specs=(tile_rows, tile_texts, smem, smem, smem),
+        scratch_shapes=[buf(rows)],
+        compiler_params=pltpu.CompilerParams(vmem_limit_bytes=40 * 1024 * 1024),
+    )(scale, back, text_in, gt, p_t)
 
 
 def solution(mesh):

time: 130 us -> 124 us (0.954)
  between operations: 7.12 us -> 1.94 us
  local copies, waits for them, and re-layouts: 3.93 us -> 5.29 us
    pallas_call x1 -> x2, Pallas kernels: 118 us -> 117 us  [the longest x1 113 us: local(): pl.pallas_call(functools.partial(kernel, n_dp), out_shape=(jax.ShapeDtype...]
    unnamed x4 -> x8, local copies, waits for them, and re-layouts: 3.93 us -> 5.29 us
where the time goes in v2:
time: 124 us
  Pallas kernels  117 us (94%)
  local copies, waits for them, and re-layouts  5.29 us (4%)
  between operations  1.94 us (2%)
    pallas_call x1, Pallas kernels, local(): pl.pallas_call(functools.partial(kernel, n_dp), out_shape=(jax.ShapeDtype...  113 us
    unnamed x8, local copies, waits for them, and re-layouts  5.29 us
    pallas_call x1, Pallas kernels, local(): pl.pallas_call(functools.partial(finish, n_dp, pairs, per_chip), out_shap...  3.38 us

profile of v2, /device:TPU:1, one launch (start us, length us, event | category | flops | bytes accessed | tf_op | source)
XLA Modules:
  0.0 123.7 jit_solution(2425133047474210450)
XLA Ops:
  1.9 113.1 %shard_map.101 = (bf16[64,16,640]{2,1,0:T(8,128)(2,1)}, bf16[512,1152]{1,0:T(8,128)(2,1)}, f32[512,1152]{1,0:T(8,128)}, bf16[512,512]{1,0:T(8,128)(2,1)}) custom-call(f32[1,1]{1,0:T(1,128)} %bitcast.4.scale_ref, f32[1,1]{1,0:T(1,128)} %bitcast.6.bias_ref, s32[1,512]{1,0:T(1,128)} %bitcast.7, s32[1,256]{1,0:T(1,128)} %bitcast.8, ...), custom_call_target="tpu_custom_call" | custom-call | tf_op jit(solution)/shard_map/pallas_call | solution.py:482
  115.1 0.0 copy-start
  115.1 1.7 %copy-done = f32[512,1152]{1,0:T(8,128)S(1)} copy-done((f32[512,1152]{1,0:T(8,128)S(1)}, f32[512,1152]{1,0:T(8,128)}, u32[]{:S(2)}) %copy-start) | copy-done | bytes 2359320
  116.7 0.0 copy-start.1
  116.7 1.3 %copy-done.1 = bf16[64,16,640]{2,1,0:T(8,128)(2,1)S(1)} copy-done((bf16[64,16,640]{2,1,0:T(8,128)(2,1)S(1)}, bf16[64,16,640]{2,1,0:T(8,128)(2,1)}, u32[]{:S(2)}) %copy-start.1) | copy-done | bytes 1310744
  118.1 0.0 copy-start.2
  118.1 1.3 %copy-done.2 = bf16[512,1152]{1,0:T(8,128)(2,1)S(1)} copy-done((bf16[512,1152]{1,0:T(8,128)(2,1)S(1)}, bf16[512,1152]{1,0:T(8,128)(2,1)}, u32[]{:S(2)}) %copy-start.2) | copy-done | bytes 1179672
  119.3 0.0 copy-start.3
  119.3 1.0 copy-done.3
  120.4 3.4 %shard_map.102 = (bf16[512,1152]{1,0:T(8,128)(2,1)}, f32[512,1152]{1,0:T(8,128)}, f32[1]{0:T(128)}, f32[1]{0:T(128)}, f32[1]{0:T(128)}) custom-call(f32[1,1]{1,0:T(1,128)} %bitcast.5.scale_ref, bf16[64,16,640]{2,1,0:T(8,128)(2,1)S(1)} %copy-done.1, bf16[512,1152]{1,0:T(8,128)(2,1)S(1)} %copy-done.2, f32[512,1152]{1,0:T(8,128)S(1)} %copy-done, ...), custom_call_target="tpu_custom_call" | custom-call | tf_op jit(solution)/shard_map/pallas_call | solution.py:544
Async XLA Ops:
  115.1 1.7 %copy-start = (f32[512,1152]{1,0:T(8,128)S(1)}, f32[512,1152]{1,0:T(8,128)}, u32[]{:S(2)}) copy-start(f32[512,1152]{1,0:T(8,128)} %get-tuple-element.11.gt_in_ref) | copy-start | bytes 7077892
  116.7 1.3 %copy-start.1 = (bf16[64,16,640]{2,1,0:T(8,128)(2,1)S(1)}, bf16[64,16,640]{2,1,0:T(8,128)(2,1)}, u32[]{:S(2)}) copy-start(bf16[64,16,640]{2,1,0:T(8,128)(2,1)} %get-tuple-element.9.back_ref) | copy-start | bytes 3932164
  118.1 1.3 %copy-start.2 = (bf16[512,1152]{1,0:T(8,128)(2,1)S(1)}, bf16[512,1152]{1,0:T(8,128)(2,1)}, u32[]{:S(2)}) copy-start(bf16[512,1152]{1,0:T(8,128)(2,1)} %get-tuple-element.10.text_in_ref) | copy-start | bytes 3538948
  119.3 1.0 copy-start.3

commit v3 on v2

--- a/solution.py
+++ b/solution.py
@@ -10,6 +10,9 @@
 STOPS = 4
 LANES = 128
 MESH = pl.DeviceIdType.MESH
+STRIDE, UNSTRIDE = 27, 19
+LOG2E = 1.4426950408889634
+LN2 = 0.6931471805599453
 F32 = jnp.float32
 BF16 = jnp.bfloat16
 
@@ -20,6 +23,17 @@
 
 def mm(a, b):
     return lax.dot_general(a, b, (((1,), (0,)), ((), ())), preferred_element_type=F32)
+
+
+def mm_tn(a, b):
+    return lax.dot_general(a, b, (((0,), (0,)), ((), ())), preferred_element_type=F32)
+
+
+def fold(x, op):
+    while x.shape[0] > 8:
+        n = x.shape[0] // 2
+        x = op(x[:n], x[n:])
+    return x
 
 
 def mm_nt(a, b):
@@ -48,7 +62,8 @@
     sl,
     lab,
     wt,
-    wn,
+    inner_ref,
+    sums_ref,
     own,
     own_in,
     pre,
@@ -133,7 +148,7 @@
     slot_id = rest - to_sub * slots
     even = (group & 1) == 0
     to_m = lax.div((group + (n_dp - 1)) & (n_dp - 1), 2)
-    rel = (to_m * 2 + to_sub - chip + (chips - 1)) & (chips - 1)
+    rel = ((to_m * 2 + to_sub - chip + chips) * UNSTRIDE + (chips - 1)) & (chips - 1)
     rel = jnp.where(valid, rel, -1)
     onehot = rel == iota((chips, rows), 0)
     earlier = (iota((rows, rows), 0) < iota((rows, rows), 1)).astype(F32).astype(BF16)
@@ -180,7 +195,7 @@
                 dst_ref=into.at[k],
                 send_sem=a2a_send.at[which_sem],
                 recv_sem=a2a_recv.at[which_sem],
-                device_id=chip_dev(chip + sign * (k + 1)),
+                device_id=chip_dev(chip + sign * lax.rem((k + 1) * STRIDE, chips)),
                 device_id_type=MESH,
             ).start()
             return carry
@@ -237,11 +252,11 @@
     half_o = pl.ds(pl.multiple_of((1 - c) * half, half), half)
 
     def ext1(which_half):
-        return sl.at[0, which_half]
+        return sl.at[which_half]
 
     ext1_copy = remote(home.at[half_c], ext1(half_c), 2, m_dev(-1))
     ext1_copy.start()
-    ext2_copy = remote(home.at[pl.ds(slots, slots)], sl.at[1], 3, m_dev(1 - 2 * c))
+    ext2_copy = remote(home.at[pl.ds(slots, slots)], sl.at[pl.ds(slots, slots)], 3, m_dev(1 - 2 * c))
 
     @pl.when(c == 0)
     def _():
@@ -250,129 +265,131 @@
     text_copy.wait()
 
     factor = scale_ref[...]
-    offset = bias_ref[...]
-
-    def slot_rows(o):
-        if o < 2:
-            return home[o * slots : (o + 1) * slots, :]
-        return sl[o - 2]
-
-    def group_terms(o, sums):
-        labels = lab[o]
+    factor2 = factor * LOG2E
+    offset2 = bias_ref[...] * LOG2E
+    sums_ref[...] = jnp.zeros_like(sums_ref)
+
+    def add(x, y):
+        return x + y
+
+    def scores(o, n, slot_rows):
+        wide = n * slots
+        inner_ref[:, :wide] = mm_nt(text_ref[...], slot_rows)
+        labels = lab[o] if n == 1 else jnp.concatenate([lab[o], lab[o + 1]], axis=1)
 
         def chunk(j, sums):
             at = pl.multiple_of(j * t_tile, t_tile)
-            inner = mm_nt(text_ref[pl.ds(at, t_tile), :], slot_rows(o))
-            logits = factor * inner + offset
-            e = jnp.exp(-jnp.abs(logits))
+            inner = inner_ref[pl.ds(at, t_tile), :wide]
+            logits = factor2 * inner + offset2
+            e = jnp.exp2(-jnp.abs(logits))
             u = 1.0 + e
-            r = 1.0 / u
-            log1p = jnp.log(u) + (e - (u - 1.0)) * r
-            positive = labels == iota((t_tile, slots), 0) + (d * texts + at)
+            r = pl.reciprocal(u, approx=True)
+            r = r * (2.0 - u * r)
             sig = jnp.where(logits >= 0.0, r, e * r)
+            positive = iota((t_tile, wide), 0) == labels - (d * texts + at)
             grad = jnp.where(positive, sig - 1.0, sig)
-            loss = jnp.maximum(logits, 0.0) + log1p - jnp.where(positive, logits, 0.0)
-            weights = grad.astype(BF16)
-            wt[pl.ds(at, t_tile), o * slots : (o + 1) * slots] = weights
-            wn[o, :, pl.ds(at, t_tile)] = jnp.transpose(weights)
+            linear = jnp.maximum(jnp.where(positive, -logits, logits), 0.0)
+            wt[pl.ds(at, t_tile), o * slots : o * slots + wide] = grad.astype(BF16)
+            log_u = jnp.log(fold(u, lambda x, y: x * y))
             return (
-                sums[0] + jnp.sum(loss, axis=0, keepdims=True),
-                sums[1] + jnp.sum(grad * inner, axis=0, keepdims=True),
-                sums[2] + jnp.sum(grad, axis=0, keepdims=True),
+                sums[0] + fold(linear, add),
+                sums[1] + log_u + fold(e - (u - 1.0), add),
+                sums[2] + fold(grad * inner, add),
+                sums[3] + fold(grad, add),
             )
 
-        return lax.fori_loop(0, texts // t_tile, chunk, sums)
-
-    c_tile = 384 if columns % 384 == 0 else LANES
-
-    def image_term(out, base, o, cast=None):
-        def tile(j, carry):
-            at = pl.ds(pl.multiple_of(j * c_tile, c_tile), c_tile)
-            res = mm(wn[o], text_ref[:, at])
-            out[base : base + slots, at] = res if cast is None else res.astype(cast)
-            return carry
-
-        lax.fori_loop(0, columns // c_tile, tile, 0)
+        sums = lax.fori_loop(0, texts // t_tile, chunk, (jnp.zeros((8, wide), F32),) * 4)
+        for k in range(4):
+            for g in range(n):
+                sums_ref[k] += sums[k][:, g * slots : (g + 1) * slots]
+
+    def image_terms(o, n):
+        return mm_tn(wt[:, o * slots : (o + n) * slots], text_ref[...])
 
     n_text = text_half // t_tile
-
-    def text_rows(base, j):
-        return pl.ds(pl.multiple_of(base + j * t_tile, t_tile), t_tile)
-
-    def text_part(base, j, first, last, rows_of):
-        return mm(wt[text_rows(base, j), first * slots : last * slots], rows_of())
-
-    mine, theirs = s * text_half, (1 - s) * text_half
-
-    sums = (jnp.zeros((1, slots), F32),) * 3
-    sums = group_terms(0, sums)
-    sums = group_terms(1, sums)
+    mine = pl.ds(pl.multiple_of(s * text_half, text_half), text_half)
+    theirs = pl.ds(pl.multiple_of((1 - s) * text_half, text_half), text_half)
+
+    scores(0, 2, home[...])
 
     @pl.when(c == 1)
     def _():
         ext2_copy.start()
 
-    image_term(own, 0, 0)
-    image_term(own, slots, 1)
+    own[...] = image_terms(0, 2)
     own_copy = remote(own, own_in, 4, partner)
     own_copy.start()
-    for j in range(n_text):
-        here = pl.ds(j * t_tile, t_tile)
-        text_sum[here, :] = text_part(theirs, j, 0, 2, lambda: home[...])
+    text_sum[...] = mm(wt[theirs, : 2 * slots], home[...])
+    gt[...] = mm(wt[mine, : 2 * slots], home[...])
 
     ext1_copy.wait_recv()
     ext1_fwd = remote(ext1(half_c), ext1(half_c), 5, partner)
     ext1_fwd.start()
+    pre_copy = remote(pre.at[half_o], pre_in, 6, partner)
+    ret1_copy = remote(ret1_out, ret1.at[half_c], 8, m_dev(1))
+    ret2_copy = remote(ret2_out, ret2, 7, m_dev(2 * c - 1))
+    text_copies = []
     for j in range(n_text):
         here = pl.ds(j * t_tile, t_tile)
-        gt[here, :] = text_part(mine, j, 0, 2, lambda: home[...])
-    ext1_fwd.wait_recv()
-    sums = group_terms(2, sums)
-    image_term(pre, 0, 2)
-    pre_copy = remote(pre.at[half_o], pre_in, 6, partner)
-    pre_copy.start()
-    for j in range(n_text):
-        here = pl.ds(j * t_tile, t_tile)
-        text_sum[here, :] += text_part(theirs, j, 2, 3, lambda: sl[0])
-    pre_copy.wait_recv()
-    ret1_out[...] = (pre[half_c, :] + pre_in[...]).astype(BF16)
-    ret1_copy = remote(ret1_out, ret1.at[half_c], 8, m_dev(1))
-    ret1_copy.start()
-
-    ext2_copy.wait_recv()
-    sums = group_terms(3, sums)
-    text_copies = []
-
-    def send_text(j):
-        here = pl.ds(j * t_tile, t_tile)
-        text_out[here, :] = (
-            text_sum[here, :] + text_part(theirs, j, 3, 4, lambda: sl[1])
-        ).astype(BF16)
-        copy = remote(text_out.at[here], text_in.at[here], 15 + j, across)
-        copy.start()
-        text_copies.append(copy)
-
-    send_text(0)
-    image_term(ret2_out, 0, 3, BF16)
-    ret2_copy = remote(ret2_out, ret2, 7, m_dev(2 * c - 1))
-    ret2_copy.start()
-    for j in range(1, n_text):
-        send_text(j)
+        text_copies.append(remote(text_out.at[here], text_in.at[here], 15 + j, across))
+
+    def send_text(o):
+        for j in range(n_text):
+            here = pl.ds(j * t_tile, t_tile)
+            at = pl.ds(pl.multiple_of((1 - s) * text_half + j * t_tile, t_tile), t_tile)
+            late = mm(wt[at, o * slots :], sl[(o - 2) * slots :, :])
+            text_out[here, :] = (text_sum[here, :] + late).astype(BF16)
+            text_copies[j].start()
+
+    def send_pre():
+        pre[...] = image_terms(2, 1)
+        pre_copy.start()
+
+    def send_ret1():
+        pre_copy.wait_recv()
+        ret1_out[...] = (pre[half_c, :] + pre_in[...]).astype(BF16)
+        ret1_copy.start()
+
+    def send_ret2():
+        ret2_out[...] = image_terms(3, 1).astype(BF16)
+        ret2_copy.start()
+
+    @pl.when(c == 0)
+    def _():
+        ext2_copy.wait_recv()
+        scores(3, 1, sl[slots:, :])
+        ext1_fwd.wait_recv()
+        scores(2, 1, sl[:slots, :])
+        send_text(2)
+        send_pre()
+        send_ret1()
+        send_ret2()
+
+    @pl.when(c == 1)
+    def _():
+        ext1_fwd.wait_recv()
+        scores(2, 1, sl[:slots, :])
+        send_pre()
+        text_sum[...] += mm(wt[theirs, 2 * slots : 3 * slots], sl[:slots, :])
+        ext2_copy.wait_recv()
+        scores(3, 1, sl[slots:, :])
+        send_ret1()
+        send_ret2()
+        send_text(3)
+
+    gt[...] += mm(wt[mine, 2 * slots :], sl[...])
+    gt_copy = pltpu.make_async_copy(gt, gt_hbm, local_sem.at[5])
+    gt_copy.start()
 
     lane = iota((8, LANES), 1)
-    totals = [jnp.sum(x, axis=1, keepdims=True) for x in sums]
+    totals = [
+        jnp.sum(x, keepdims=True)
+        for x in (LN2 * sums_ref[0] + sums_ref[1], sums_ref[2], sums_ref[3])
+    ]
     kind = lax.rem(lane, 3)
     stat[...] = jnp.where(kind == 0, totals[0], jnp.where(kind == 1, totals[1], totals[2]))
     stat_copy = remote(stat, stat_in, 9, partner)
     stat_copy.start()
-
-    for j in range(n_text):
-        here = pl.ds(j * t_tile, t_tile)
-        gt[here, :] += text_part(mine, j, 2, 3, lambda: sl[0]) + text_part(
-            mine, j, 3, 4, lambda: sl[1]
-        )
-    gt_copy = pltpu.make_async_copy(gt, gt_hbm, local_sem.at[5])
-    gt_copy.start()
 
     ret1_copy.wait_recv()
     ret1_fwd = remote(ret1.at[half_c], ret1.at[half_c], 13, partner)
@@ -449,7 +466,7 @@
         )
         chip = lax.div(lax.axis_index("dp"), 2) * 2 + lax.axis_index("sub")
         sums_in = back_ref[:, per_chip:, tail:].astype(F32)[:, 0, :].astype(BF16)
-        source = (chip + 1 + iota((chips, chips), 1)) & (chips - 1)
+        source = (chip + (iota((chips, chips), 1) + 1) * STRIDE) & (chips - 1)
         order = (source == iota((chips, chips), 0)).astype(F32).astype(BF16)
         total = jnp.sum(mm(order, sums_in), axis=0, keepdims=True)
         lane = iota((1, LANES), 1)
@@ -497,10 +514,11 @@
             buf(2 * slots),
             buf(2 * slots),
             buf(2 * slots),
-            pltpu.VMEM((2, slots, columns), BF16),
+            buf(2 * slots),
             pltpu.VMEM((4, 1, slots), jnp.int32),
             pltpu.VMEM((texts, 4 * slots), BF16),
-            pltpu.VMEM((4, slots, texts), BF16),
+            pltpu.VMEM((texts, 2 * slots), F32),
+            pltpu.VMEM((4, 8, slots), F32),
             buf(2 * slots, F32),
             buf(2 * slots, F32),
             buf(slots, F32),
@@ -560,7 +578,7 @@
         ],
         out_specs=(tile_rows, tile_texts, smem, smem, smem),
         scratch_shapes=[buf(rows)],
-        compiler_params=pltpu.CompilerParams(vmem_limit_bytes=40 * 1024 * 1024),
+        compiler_params=pltpu.CompilerParams(vmem_limit_bytes=60 * 1024 * 1024),
     )(scale, back, text_in, gt, p_t)
 
 

time: 124 us -> 116 us (0.935); the launches traced: 124 us -> 114 us
  local copies, waits for them, and re-layouts: 5.29 us -> 0 us
  Pallas kernels: 117 us -> 112 us
    pallas_call x1, Pallas kernels: 113 us -> 106 us  [local(): pl.pallas_call(functools.partial(kernel, n_dp), out_shape=(jax.ShapeDtype...]
    unnamed x8 -> x0, local copies, waits for them, and re-layouts: 5.29 us -> none
    pallas_call x1, Pallas kernels: 3.38 us -> 6.16 us  [local(): pl.pallas_call(functools.partial(finish, n_dp, pairs, per_chip), out_shap...]
where the time goes in v3:
time: 116 us; the launch traced here: 114 us
  Pallas kernels  112 us (97%)
  between operations  1.93 us (2%)
    pallas_call x1, Pallas kernels, local(): pl.pallas_call(functools.partial(kernel, n_dp), out_shape=(jax.ShapeDtype...  106 us
    pallas_call x1, Pallas kernels, local(): pl.pallas_call(functools.partial(finish, n_dp, pairs, per_chip), out_shap...  6.16 us

profile of v3, /device:TPU:1, one launch (start us, length us, event | category | flops | bytes accessed | tf_op | source)
XLA Modules:
  0.0 113.8 jit_solution(16938542539607418001)
XLA Ops:
  1.9 105.7 %shard_map.101 = (bf16[64,16,640]{2,1,0:T(8,128)(2,1)}, bf16[512,1152]{1,0:T(8,128)(2,1)}, f32[512,1152]{1,0:T(8,128)}, bf16[512,512]{1,0:T(8,128)(2,1)}) custom-call(f32[1,1]{1,0:T(1,128)} %bitcast.4.scale_ref, f32[1,1]{1,0:T(1,128)} %bitcast.6.bias_ref, s32[1,512]{1,0:T(1,128)} %bitcast.7, s32[1,256]{1,0:T(1,128)} %bitcast.8, ...), custom_call_target="tpu_custom_call" | custom-call | tf_op jit(solution)/shard_map/pallas_call | solution.py:499
  107.6 6.2 %shard_map.102 = (bf16[512,1152]{1,0:T(8,128)(2,1)}, f32[512,1152]{1,0:T(8,128)}, f32[1]{0:T(128)}, f32[1]{0:T(128)}, f32[1]{0:T(128)}) custom-call(f32[1,1]{1,0:T(1,128)} %bitcast.5.scale_ref, bf16[64,16,640]{2,1,0:T(8,128)(2,1)} %get-tuple-element.9.back_ref, bf16[512,1152]{1,0:T(8,128)(2,1)} %get-tuple-element.10.text_in_ref, ...), custom_call_target="tpu_custom_call" | custom-call | tf_op jit(solution)/shard_map/pallas_call | solution.py:562

commit v4 on v3

--- a/solution.py
+++ b/solution.py
@@ -104,6 +104,8 @@
     m = lax.div(d, 2)
     c = lax.rem(d, 2)
     chip = m * 2 + s
+    upper = lax.div(m, n_m // 2)
+    half_here = lax.rem(s + upper, 2)
     partner = (m * 2 + (1 - c), s)
     across = (d, 1 - s)
 
@@ -112,10 +114,15 @@
         return (lax.div(i, 2) * 2 + c, lax.rem(i, 2))
 
     def m_dev(step):
-        return (lax.rem(m + step + n_m, n_m) * 2 + c, s)
-
-    def dp_dev(step):
-        return (lax.rem(d + step + n_dp, n_dp), s)
+        there = lax.rem(m + step + n_m, n_m)
+        return (there * 2 + c, lax.rem(half_here + lax.div(there, n_m // 2), 2))
+
+    def labels_to(step):
+        there = lax.rem(d - step + n_dp, n_dp)
+        return (there, lax.rem(s + lax.div(there, n_dp // 2), 2))
+
+    def labels_from(step):
+        return (lax.rem(d + step, n_dp), half_here)
 
     text_copy = pltpu.make_async_copy(text_hbm, text_ref, local_sem.at[3])
     text_copy.start()
@@ -127,7 +134,7 @@
         return carry
 
     lax.fori_loop(1, chips, greet, 0)
-    for dev in (partner, dp_dev(1), dp_dev(3)):
+    for dev in (partner, labels_from(1), labels_from(3)):
         pl.semaphore_signal(barrier, inc=1, device_id=dev, device_id_type=MESH)
 
     def remote(src, dst, k, dev):
@@ -148,6 +155,7 @@
     slot_id = rest - to_sub * slots
     even = (group & 1) == 0
     to_m = lax.div((group + (n_dp - 1)) & (n_dp - 1), 2)
+    to_sub = (to_sub + lax.div(to_m, n_m // 2)) & 1
     rel = ((to_m * 2 + to_sub - chip + chips) * UNSTRIDE + (chips - 1)) & (chips - 1)
     rel = jnp.where(valid, rel, -1)
     onehot = rel == iota((chips, rows), 0)
@@ -180,13 +188,22 @@
     pl.semaphore_wait(barrier, chips - 1 + 3)
 
     lab_copies = [
-        remote(labels_ref, lab.at[slot], 9 + step, dp_dev(-step))
+        remote(labels_ref, lab.at[slot], 9 + step, labels_to(step))
         for step, slot in ((1, 1 - c), (2, 1 + c), (3, 3 - c))
     ]
     for copy in lab_copies:
         copy.start()
     lab_own = pltpu.make_async_copy(labels_ref, lab.at[3 - 3 * c], local_sem.at[0])
-    lab_own.start()
+    lab_swap = remote(labels_ref, lab.at[3 - 3 * c], 20, across)
+
+    @pl.when(upper == 0)
+    def _():
+        lab_own.start()
+
+    @pl.when(upper == 1)
+    def _():
+        lab_swap.start()
+
 
     def all_start(buf, into, which_sem, sign, lo, hi):
         def step(k, carry):
@@ -241,7 +258,15 @@
         copy = remote(part.at[here], part_in.at[here], g, partner)
         copy.start()
         part_copies.append(copy)
-    lab_own.wait()
+
+    @pl.when(upper == 0)
+    def _():
+        lab_own.wait()
+
+    @pl.when(upper == 1)
+    def _():
+        lab_swap.wait()
+
     for copy in lab_copies:
         copy.wait()
     for g in range(2):
@@ -555,7 +580,7 @@
         images,
         text_embeds,
     )
-    tiles = 4
+    tiles = 2
     tile_rows = pl.BlockSpec((rows // tiles, columns), lambda i: (i, 0))
     tile_texts = pl.BlockSpec((texts // 2 // tiles, columns), lambda i: (i, 0))
     scalar = jax.ShapeDtypeStruct((1,), F32)

time: 116 us -> 100 us (0.86); the launches traced: 114 us -> 99.8 us
  Pallas kernels: 112 us -> 97.9 us
    pallas_call x1, Pallas kernels: 106 us -> 92.7 us  [local(): pl.pallas_call(functools.partial(kernel, n_dp), out_shape=(jax.ShapeDtype...]
where the time goes in v4:
time: 100 us; the launch traced here: 99.8 us
  Pallas kernels  97.9 us (98%)
  between operations  1.93 us (2%)
    pallas_call x1, Pallas kernels, local(): pl.pallas_call(functools.partial(kernel, n_dp), out_shape=(jax.ShapeDtype...  92.7 us
    pallas_call x1, Pallas kernels, local(): pl.pallas_call(functools.partial(finish, n_dp, pairs, per_chip), out_shap...  5.19 us

profile of v4, /device:TPU:1, one launch (start us, length us, event | category | flops | bytes accessed | tf_op | source)
XLA Modules:
  0.0 99.8 jit_solution(16590984571464322824)
XLA Ops:
  1.9 92.7 %shard_map.101 = (bf16[64,16,640]{2,1,0:T(8,128)(2,1)}, bf16[512,1152]{1,0:T(8,128)(2,1)}, f32[512,1152]{1,0:T(8,128)}, bf16[512,512]{1,0:T(8,128)(2,1)}) custom-call(f32[1,1]{1,0:T(1,128)} %bitcast.4.scale_ref, f32[1,1]{1,0:T(1,128)} %bitcast.6.bias_ref, s32[1,512]{1,0:T(1,128)} %bitcast.7, s32[1,256]{1,0:T(1,128)} %bitcast.8, ...), custom_call_target="tpu_custom_call" | custom-call | tf_op jit(solution)/shard_map/pallas_call | solution.py:524
  94.6 5.2 %shard_map.102 = (bf16[512,1152]{1,0:T(8,128)(2,1)}, f32[512,1152]{1,0:T(8,128)}, f32[1]{0:T(128)}, f32[1]{0:T(128)}, f32[1]{0:T(128)}) custom-call(f32[1,1]{1,0:T(1,128)} %bitcast.5.scale_ref, bf16[64,16,640]{2,1,0:T(8,128)(2,1)} %get-tuple-element.9.back_ref, bf16[512,1152]{1,0:T(8,128)(2,1)} %get-tuple-element.10.text_in_ref, ...), custom_call_target="tpu_custom_call" | custom-call | tf_op jit(solution)/shard_map/pallas_call | solution.py:587

commit v5 on v4

--- a/solution.py
+++ b/solution.py
@@ -48,10 +48,11 @@
     labels_ref,
     images_ref,
     text_hbm,
-    back_recv,
+    back_in,
+    stats_in,
     text_in,
     gt_hbm,
-    p_hbm,
+    placed_hbm,
     text_ref,
     send,
     recv,
@@ -73,11 +74,11 @@
     ret2_out,
     ret2,
     ret2b,
-    slot_grad,
+    grad_rows,
     text_sum,
     text_out,
     gt,
-    p_t,
+    placed_ref,
     q_t,
     stat,
     stat_in,
@@ -124,7 +125,7 @@
     def labels_from(step):
         return (lax.rem(d + step, n_dp), half_here)
 
-    text_copy = pltpu.make_async_copy(text_hbm, text_ref, local_sem.at[3])
+    text_copy = pltpu.make_async_copy(text_hbm, text_ref, local_sem.at[7])
     text_copy.start()
 
     barrier = pltpu.get_barrier_semaphore()
@@ -164,11 +165,10 @@
     rank = mm(onehot_f.astype(BF16), earlier)
     within = jnp.sum(onehot_f * rank, axis=0, keepdims=True)
     placed = jnp.where(valid, rel.astype(F32) * float(per_chip) + within, -1.0)
-    placed_col = jnp.transpose(jnp.broadcast_to(placed, (LANES, rows)))[:, :1].astype(jnp.int32)
-    p_t[...] = (placed_col == iota((rows, rows), 1)).astype(F32).astype(BF16)
-    p_copy = pltpu.make_async_copy(p_t, p_hbm, local_sem.at[4])
-    p_copy.start()
     placed_int = placed.astype(jnp.int32)
+    placed_ref[...] = placed_int
+    placed_copy = pltpu.make_async_copy(placed_ref, placed_hbm, local_sem.at[4])
+    placed_copy.start()
     id_plus = (slot_id + 1).astype(F32)
     id_odd = jnp.where(valid & jnp.logical_not(even), id_plus, 0.0)
     id_even = jnp.where(valid & even, id_plus, 0.0)
@@ -193,7 +193,7 @@
     ]
     for copy in lab_copies:
         copy.start()
-    lab_own = pltpu.make_async_copy(labels_ref, lab.at[3 - 3 * c], local_sem.at[0])
+    lab_own = pltpu.make_async_copy(labels_ref, lab.at[3 - 3 * c], local_sem.at[6])
     lab_swap = remote(labels_ref, lab.at[3 - 3 * c], 20, across)
 
     @pl.when(upper == 0)
@@ -205,11 +205,28 @@
         lab_swap.start()
 
 
-    def all_start(buf, into, which_sem, sign, lo, hi):
+    def all_start(src, dst, own_src, own_dst, total, which_sem, sign):
         def step(k, carry):
+            to = lax.rem(chip + sign * lax.rem((k + 1) * STRIDE, chips) + chips, chips)
+            swaps = lax.rem(to, 2) + s + lax.div(to, chips // 2) + upper
+
+            @pl.when(lax.rem(swaps, 2) == carry)
+            def _():
+                pltpu.make_async_remote_copy(
+                    src_ref=src(k),
+                    dst_ref=dst(k),
+                    send_sem=a2a_send.at[which_sem],
+                    recv_sem=a2a_recv.at[which_sem],
+                    device_id=chip_dev(to),
+                    device_id_type=MESH,
+                ).start()
+
+            return carry
+
+        def step_any(k, carry):
             pltpu.make_async_remote_copy(
-                src_ref=buf.at[k],
-                dst_ref=into.at[k],
+                src_ref=src(k),
+                dst_ref=dst(k),
                 send_sem=a2a_send.at[which_sem],
                 recv_sem=a2a_recv.at[which_sem],
                 device_id=chip_dev(chip + sign * lax.rem((k + 1) * STRIDE, chips)),
@@ -217,28 +234,27 @@
             ).start()
             return carry
 
-        lax.fori_loop(lo, min(hi, chips - 1), step, 0)
-
-    def own_start(buf, into, which_sem):
-        copy = pltpu.make_async_copy(
-            buf.at[chips - 1], into.at[chips - 1], local_sem.at[1 + which_sem]
-        )
-        copy.start()
-        return copy
-
-    def all_desc(buf, into, which_sem):
-        return pltpu.make_async_remote_copy(
-            src_ref=buf.at[pl.ds(0, chips - 1)],
-            dst_ref=into.at[pl.ds(0, chips - 1)],
+        if which_sem == 0:
+            lax.fori_loop(0, chips - 1, step_any, 0)
+        else:
+            for turn in range(2):
+                lax.fori_loop(0, chips - 1, step, turn)
+        own_copy = pltpu.make_async_copy(own_src, own_dst, local_sem.at[which_sem])
+        own_copy.start()
+        all_copy = pltpu.make_async_remote_copy(
+            src_ref=total.at[pl.ds(0, chips - 1)],
+            dst_ref=total.at[pl.ds(0, chips - 1)],
             send_sem=a2a_send.at[which_sem],
             recv_sem=a2a_recv.at[which_sem],
             device_id=partner,
             device_id_type=MESH,
         )
-
-    all_start(send, recv, 0, 1, 0, chips)
-    out_own = own_start(send, recv, 0)
-    out_all = all_desc(send, recv, 0)
+        return own_copy, all_copy
+
+    last = chips - 1
+    out_own, out_all = all_start(
+        lambda k: send.at[k], lambda k: recv.at[k], send.at[last], recv.at[last], recv, 0, 1
+    )
     out_own.wait()
     out_all.wait_recv()
 
@@ -337,15 +353,15 @@
 
     scores(0, 2, home[...])
 
-    @pl.when(c == 1)
-    def _():
-        ext2_copy.start()
-
     own[...] = image_terms(0, 2)
     own_copy = remote(own, own_in, 4, partner)
     own_copy.start()
+
+    @pl.when(c == 1)
+    def _():
+        ext2_copy.start()
+
     text_sum[...] = mm(wt[theirs, : 2 * slots], home[...])
-    gt[...] = mm(wt[mine, : 2 * slots], home[...])
 
     ext1_copy.wait_recv()
     ext1_fwd = remote(ext1(half_c), ext1(half_c), 5, partner)
@@ -402,63 +418,58 @@
         send_ret2()
         send_text(3)
 
-    gt[...] += mm(wt[mine, 2 * slots :], sl[...])
-    gt_copy = pltpu.make_async_copy(gt, gt_hbm, local_sem.at[5])
-    gt_copy.start()
-
-    lane = iota((8, LANES), 1)
+    lane = iota((1, LANES), 1)
     totals = [
         jnp.sum(x, keepdims=True)
         for x in (LN2 * sums_ref[0] + sums_ref[1], sums_ref[2], sums_ref[3])
     ]
-    kind = lax.rem(lane, 3)
-    stat[...] = jnp.where(kind == 0, totals[0], jnp.where(kind == 1, totals[1], totals[2]))
+    stat[...] = jnp.where(lane == 0, totals[0], jnp.where(lane == 1, totals[1], totals[2]))
     stat_copy = remote(stat, stat_in, 9, partner)
     stat_copy.start()
+    gt[...] = mm(wt[mine, : 2 * slots], home[...]) + mm(wt[mine, 2 * slots :], sl[...])
+    gt_copy = pltpu.make_async_copy(gt, gt_hbm, local_sem.at[5])
+    gt_copy.start()
+    stat_copy.wait()
+    stat[...] = stat[...] + stat_in[...]
+    own_stats, all_stats = all_start(
+        lambda k: stat, lambda k: stats_in.at[chip], stat, stats_in.at[chip], stats_in, 2, 1
+    )
 
     ret1_copy.wait_recv()
     ret1_fwd = remote(ret1.at[half_c], ret1.at[half_c], 13, partner)
     ret1_fwd.start()
+    own_copy.wait_recv()
+    ret1_fwd.wait_recv()
+    total = own[:slots, :] + own_in[:slots, :] + ret1[...].astype(F32)
+    grad_rows[:slots, :] = (factor * total).astype(BF16)
     ret2_copy.wait_recv()
     ret2_fwd = remote(ret2, ret2b, 14, partner)
     ret2_fwd.start()
-    own_copy.wait_recv()
-    stat_copy.wait_recv()
-
-    value = stat[...] + stat_in[...]
-    top = value.astype(BF16).astype(F32)
-    middle = (value - top).astype(BF16).astype(F32)
-    low = value - top - middle
-    payload = jnp.where(lane < 3, top, jnp.where(lane < 6, middle, jnp.where(lane < 9, low, 0.0)))
-
-    ret1_fwd.wait_recv()
-    odd = own[:slots, :] + own_in[:slots, :] + ret1[...].astype(F32)
-    slot_grad[:slots, :] = (factor * odd).astype(BF16)
     ret2_fwd.wait_recv()
-    evn = own[slots:, :] + own_in[slots:, :] + (ret2[...].astype(F32) + ret2b[...].astype(F32))
-    slot_grad[slots:, :] = (factor * evn).astype(BF16)
-
-    payload_rows = jnp.broadcast_to(payload[:per_chip][None], (row_tile // per_chip, per_chip, LANES))
-    for r in range(rows // row_tile):
-        n = row_tile // per_chip
-        q_rows = q_t[r * row_tile : (r + 1) * row_tile, :]
-        first = mm(q_rows, slot_grad[:, :width]).reshape(n, per_chip, width)
-        second = mm(q_rows, slot_grad[:, width:]).reshape(n, per_chip, tail)
-        second = jnp.concatenate([second, payload_rows], axis=2)
-        back[r * n : (r + 1) * n] = jnp.concatenate([first, second], axis=1).astype(BF16)
-        all_start(back, back_recv, 1, -1, r * n, (r + 1) * n)
-
-    back_own = own_start(back, back_recv, 1)
-    back_all = all_desc(back, back_recv, 1)
+    total = own[slots:, :] + own_in[slots:, :] + (ret2[...].astype(F32) + ret2b[...].astype(F32))
+    grad_rows[slots:, :] = (factor * total).astype(BF16)
+
+    parts = 4 if chips >= 32 else 1
+    n = chips // parts
+    for r in range(parts):
+        out = mm(q_t[r * rows // parts : (r + 1) * rows // parts, :], grad_rows[...])
+        tiles = [
+            out[:, b : b + LANES].reshape(n, per_chip, LANES) for b in range(0, columns, LANES)
+        ]
+        back[r * n : (r + 1) * n] = jnp.concatenate(tiles, axis=1).astype(BF16)
+    own_back, all_back = all_start(
+        lambda k: back.at[k], lambda k: back_in.at[k], back.at[last], back_in.at[last], back_in, 1, -1
+    )
+
     for copy in text_copies:
         copy.wait_recv()
-    p_copy.wait()
+    placed_copy.wait()
     gt_copy.wait()
-    back_own.wait()
-    back_all.wait_recv()
-
+    own_stats.wait()
+    all_stats.wait()
+    own_back.wait()
+    all_back.wait()
     out_all.wait_send()
-    back_all.wait_send()
     for copy in (
         ext1_copy,
         ext2_copy,
@@ -467,7 +478,6 @@
         pre_copy,
         ret2_copy,
         ret1_copy,
-        stat_copy,
         ret1_fwd,
         ret2_fwd,
         *text_copies,
@@ -475,31 +485,27 @@
         copy.wait_send()
 
 
-def finish(n_dp, pairs, per_chip, scale_ref, back_ref, text_in_ref, gt_in_ref, p_ref, *rest):
-    gi_ref, gt_ref, loss_ref, gscale_ref, gbias_ref, rows_in = rest
-    chips, _, width = back_ref.shape
-    rows, columns = rows_in.shape
-    tail = columns - width
-
-    @pl.when(pl.program_id(0) == 0)
-    def _():
-        rows_in[:, :width] = (
-            back_ref[:, :per_chip, :].astype(F32).reshape(rows, width).astype(BF16)
-        )
-        rows_in[:, width:] = (
-            back_ref[:, per_chip:, :tail].astype(F32).reshape(rows, tail).astype(BF16)
-        )
-        chip = lax.div(lax.axis_index("dp"), 2) * 2 + lax.axis_index("sub")
-        sums_in = back_ref[:, per_chip:, tail:].astype(F32)[:, 0, :].astype(BF16)
-        source = (chip + (iota((chips, chips), 1) + 1) * STRIDE) & (chips - 1)
-        order = (source == iota((chips, chips), 0)).astype(F32).astype(BF16)
-        total = jnp.sum(mm(order, sums_in), axis=0, keepdims=True)
+def finish(n_dp, pairs, per_chip, scale_ref, back_ref, stats_ref, text_in_ref, gt_in_ref, *rest):
+    placed_ref, gi_ref, gt_ref, loss_ref, gscale_ref, gbias_ref, rows_in, placed_col = rest
+    tile, columns = gi_ref.shape
+    pack = rows_in.shape[0]
+    step = pl.program_id(0)
+
+    @pl.when(step == 0)
+    def _():
+        for b in range(columns // LANES):
+            block = back_ref[:, b * per_chip : (b + 1) * per_chip, :].astype(F32)
+            rows_in[:, b * LANES : (b + 1) * LANES] = block.reshape(pack, LANES).astype(BF16)
+        placed = jnp.broadcast_to(placed_ref[...].astype(F32), (LANES, placed_col.shape[0]))
+        placed_col[...] = jnp.transpose(placed).astype(jnp.int32)
+        total = jnp.sum(stats_ref[...], axis=0)
         lane = iota((1, LANES), 1)
         for k, ref in enumerate((loss_ref, gscale_ref, gbias_ref)):
-            picked = (lane < 9) & (lax.rem(lane, 3) == k)
-            ref[0] = jnp.sum(jnp.where(picked, total, 0.0)) / pairs
-
-    gi_ref[...] = mm(p_ref[...], rows_in[...]).astype(BF16)
+            ref[0] = jnp.sum(jnp.where(lane == k, total, 0.0)) / pairs
+
+    placed = placed_col[pl.ds(pl.multiple_of(step * tile, tile), tile), :1]
+    choose = (placed == iota((tile, pack), 1)).astype(F32).astype(BF16)
+    gi_ref[...] = mm(choose, rows_in[...]).astype(BF16)
     gt_ref[...] = scale_ref[...] * (gt_in_ref[...] + text_in_ref[...].astype(F32))
 
 
@@ -516,26 +522,28 @@
     smem = pl.BlockSpec(memory_space=pltpu.SMEM)
     hbm = pl.BlockSpec(memory_space=pl.ANY)
     message = pltpu.VMEM((chips, 2 * per_chip, width), BF16)
+    tiled = (chips, per_chip * columns // LANES, LANES)
 
     def buf(n, dtype=BF16):
         return pltpu.VMEM((n, columns), dtype)
 
     scale = logit_scale.reshape(1, 1)
-    back, text_in, gt, p_t = pl.pallas_call(
+    back, stats, text_in, gt, placed = pl.pallas_call(
         functools.partial(kernel, n_dp),
         out_shape=(
-            jax.ShapeDtypeStruct((chips, 2 * per_chip, width), BF16),
+            jax.ShapeDtypeStruct(tiled, BF16),
+            jax.ShapeDtypeStruct((chips, 1, LANES), F32),
             jax.ShapeDtypeStruct((texts // 2, columns), BF16),
             jax.ShapeDtypeStruct((texts // 2, columns), F32),
-            jax.ShapeDtypeStruct((rows, rows), BF16),
+            jax.ShapeDtypeStruct((1, rows), jnp.int32),
         ),
         in_specs=[vmem, vmem, vmem, vmem, vmem, hbm],
-        out_specs=(hbm, hbm, hbm, hbm),
+        out_specs=(hbm, hbm, hbm, hbm, hbm),
         scratch_shapes=[
             buf(texts),
             message,
             message,
-            message,
+            pltpu.VMEM(tiled, BF16),
             buf(2 * slots),
             buf(2 * slots),
             buf(2 * slots),
@@ -557,13 +565,13 @@
             buf(texts // 2, F32),
             buf(texts // 2),
             buf(texts // 2, F32),
-            pltpu.VMEM((rows, rows), BF16),
+            pltpu.VMEM((1, rows), jnp.int32),
             pltpu.VMEM((rows, 2 * slots), BF16),
-            pltpu.VMEM((8, LANES), F32),
-            pltpu.VMEM((8, LANES), F32),
-            pltpu.SemaphoreType.DMA((2,)),
-            pltpu.SemaphoreType.DMA((2,)),
-            pltpu.SemaphoreType.DMA((6,)),
+            pltpu.VMEM((1, LANES), F32),
+            pltpu.VMEM((1, LANES), F32),
+            pltpu.SemaphoreType.DMA((3,)),
+            pltpu.SemaphoreType.DMA((3,)),
+            pltpu.SemaphoreType.DMA((8,)),
             pltpu.SemaphoreType.DMA((24,)),
             pltpu.SemaphoreType.DMA((24,)),
         ],
@@ -597,14 +605,15 @@
         in_specs=[
             pl.BlockSpec((1, 1), lambda i: (0, 0)),
             pl.BlockSpec(back.shape, lambda i: (0, 0, 0)),
+            pl.BlockSpec(stats.shape, lambda i: (0, 0, 0)),
             tile_texts,
             tile_texts,
-            pl.BlockSpec((rows // tiles, rows), lambda i: (i, 0)),
+            pl.BlockSpec((1, rows), lambda i: (0, 0)),
         ],
         out_specs=(tile_rows, tile_texts, smem, smem, smem),
-        scratch_shapes=[buf(rows)],
+        scratch_shapes=[buf(rows), pltpu.VMEM((rows, LANES), jnp.int32)],
         compiler_params=pltpu.CompilerParams(vmem_limit_bytes=60 * 1024 * 1024),
-    )(scale, back, text_in, gt, p_t)
+    )(scale, back, stats, text_in, gt, placed)
 
 
 def solution(mesh):

time: 100 us -> 98.6 us (0.986)
  Pallas kernels: 97.9 us -> 96.3 us
    pallas_call x1, Pallas kernels: 92.7 us -> 91.6 us  [local(): pl.pallas_call(functools.partial(kernel, n_dp), out_shape=(jax.ShapeDtype...]
where the time goes in v5:
time: 98.6 us; the launch traced here: 98.2 us
  Pallas kernels  96.3 us (98%)
  between operations  1.93 us (2%)
    pallas_call x1, Pallas kernels, local(): pl.pallas_call(functools.partial(kernel, n_dp), out_shape=(jax.ShapeDtype...  91.6 us
    pallas_call x1, Pallas kernels, local(): pl.pallas_call(functools.partial(finish, n_dp, pairs, per_chip), out_shap...  4.64 us

profile of v5, /device:TPU:1, one launch (start us, length us, event | category | flops | bytes accessed | tf_op | source)
XLA Modules:
  0.0 98.2 jit_solution(4823009570033706983)
XLA Ops:
  1.9 91.6 %shard_map.101 = (bf16[64,72,128]{2,1,0:T(8,128)(2,1)}, f32[64,1,128]{2,1,0:T(1,128)}, bf16[512,1152]{1,0:T(8,128)(2,1)}, f32[512,1152]{1,0:T(8,128)}, s32[1,512]{1,0:T(1,128)}) custom-call(f32[1,1]{1,0:T(1,128)} %bitcast.4.scale_ref, f32[1,1]{1,0:T(1,128)} %bitcast.6.bias_ref, s32[1,512]{1,0:T(1,128)} %bitcast.7, s32[1,256]{1,0:T(1,128)} %bitcast.8, ...), custom_call_target="tpu_custom_call" | custom-call | tf_op jit(solution)/shard_map/pallas_call | solution.py:531
  93.6 4.6 %shard_map.102 = (bf16[512,1152]{1,0:T(8,128)(2,1)}, f32[512,1152]{1,0:T(8,128)}, f32[1]{0:T(128)}, f32[1]{0:T(128)}, f32[1]{0:T(128)}) custom-call(f32[1,1]{1,0:T(1,128)} %bitcast.5.scale_ref, bf16[64,72,128]{2,1,0:T(8,128)(2,1)} %get-tuple-element.10.back_ref, f32[64,1,128]{2,1,0:T(1,128)} %get-tuple-element.11.stats_ref, ...), custom_call_target="tpu_custom_call" | custom-call | tf_op jit(solution)/shard_map/pallas_call | solution.py:595

commit v6 on v5

--- a/solution.py
+++ b/solution.py
@@ -237,7 +237,7 @@
         if which_sem == 0:
             lax.fori_loop(0, chips - 1, step_any, 0)
         else:
-            for turn in range(2):
+            for turn in (1, 0):
                 lax.fori_loop(0, chips - 1, step, turn)
         own_copy = pltpu.make_async_copy(own_src, own_dst, local_sem.at[which_sem])
         own_copy.start()
@@ -412,11 +412,11 @@
         scores(2, 1, sl[:slots, :])
         send_pre()
         text_sum[...] += mm(wt[theirs, 2 * slots : 3 * slots], sl[:slots, :])
+        send_ret1()
         ext2_copy.wait_recv()
         scores(3, 1, sl[slots:, :])
-        send_ret1()
+        send_text(3)
         send_ret2()
-        send_text(3)
 
     lane = iota((1, LANES), 1)
     totals = [

time: 98.6 us -> 98.6 us (level)
  no operation moved by 1% of the time
where the time goes in v6:
time: 98.6 us; the launch traced here: 98.2 us
  Pallas kernels  96.3 us (98%)
  between operations  1.93 us (2%)
    pallas_call x1, Pallas kernels, local(): pl.pallas_call(functools.partial(kernel, n_dp), out_shape=(jax.ShapeDtype...  91.6 us
    pallas_call x1, Pallas kernels, local(): pl.pallas_call(functools.partial(finish, n_dp, pairs, per_chip), out_shap...  4.64 us

profile of v6, /device:TPU:1, one launch (start us, length us, event | category | flops | bytes accessed | tf_op | source)
XLA Modules:
  0.0 98.2 jit_solution(4006752093587985890)
XLA Ops:
  1.9 91.6 %shard_map.101 = (bf16[64,72,128]{2,1,0:T(8,128)(2,1)}, f32[64,1,128]{2,1,0:T(1,128)}, bf16[512,1152]{1,0:T(8,128)(2,1)}, f32[512,1152]{1,0:T(8,128)}, s32[1,512]{1,0:T(1,128)}) custom-call(f32[1,1]{1,0:T(1,128)} %bitcast.4.scale_ref, f32[1,1]{1,0:T(1,128)} %bitcast.6.bias_ref, s32[1,512]{1,0:T(1,128)} %bitcast.7, s32[1,256]{1,0:T(1,128)} %bitcast.8, ...), custom_call_target="tpu_custom_call" | custom-call | tf_op jit(solution)/shard_map/pallas_call | solution.py:531
  93.6 4.6 %shard_map.102 = (bf16[512,1152]{1,0:T(8,128)(2,1)}, f32[512,1152]{1,0:T(8,128)}, f32[1]{0:T(128)}, f32[1]{0:T(128)}, f32[1]{0:T(128)}) custom-call(f32[1,1]{1,0:T(1,128)} %bitcast.5.scale_ref, bf16[64,72,128]{2,1,0:T(8,128)(2,1)} %get-tuple-element.10.back_ref, f32[64,1,128]{2,1,0:T(1,128)} %get-tuple-element.11.stats_ref, ...), custom_call_target="tpu_custom_call" | custom-call | tf_op jit(solution)/shard_map/pallas_call | solution.py:595
